TPU v7x, 256 devices: a whole 4x4x8 slice. The times are simulated.
256 devices in a mesh: mem: 4 (over x_hi, core), pts: 64 (over z, y, x_lo).
Axes of the slice: x: 4 (x_hi: 2, x_lo: 2; x = x_hi * 2 + x_lo), y: 4, z: 8, core: 2. Of those that a mesh axis runs over, the one named last changes fastest.
Arguments:
- hidden: bfloat16 [8, 1024, 65536], P('mem', None, 'pts'), may hold values from -16 to 16
- w_first: bfloat16 [1024, 1024], replicated, may hold values from -0.1875 to 0.1875
- b_first: float32 [1024], replicated, may hold values from -3 to 3
- w_out: bfloat16 [100, 1024], replicated, may hold values from -0.1875 to 0.1875
- target: float32 [100, 65536], P(None, 'pts'), may hold values from -6 to 6
- area: float32 [65536], P('pts'), may hold values from 0.3 to 3
- var_weight: float32 [100], replicated, may hold values from 1 to 10
Outputs:
- grad_hidden: bfloat16 [8, 1024, 65536], P('mem', None, 'pts')
- grad_w_first: float32 [1024, 1024], replicated
- grad_w_out: float32 [100, 1024], replicated
- grad_b_first: float32 [1024], replicated
All inputs are finite; a program needn't handle non-finite values.
Results may differ from a plain program's by a relative error of at most 0.0084.
The roundings to bfloat16 on the way count: a program that leaves them out, or rounds other values in their place, can miss the bound.
Values sent between devices are 32-bit elements; how exact they have to be, the bound alone decides.
A program may use at most 128 MiB of HBM per device.

v0:
```python
import math

import jax
import jax.numpy as jnp
from jax import lax
from jax.sharding import PartitionSpec as P

curve = 0.044715
root_coef = 0.7978845608
delta_sq = 0.0025


def gelu_value(u):
    return 0.5 * u * (1.0 + jnp.tanh(root_coef * (u + curve * u * u * u)))


def gelu_slope(u):
    inner = jnp.tanh(root_coef * (u + curve * u * u * u))
    return 0.5 * (1.0 + inner) + 0.5 * u * (1.0 - inner * inner) * root_coef * (
        1.0 + 3.0 * curve * u * u
    )


def smooth_sign(d):
    return d / jnp.sqrt(d * d + delta_sq)


def pair_terms(own, others):
    return jnp.sum(smooth_sign(own[:, None] - others[None]), axis=1)


def per_device(hidden, w_first, b_first, w_out, target, area, var_weight):
    mem_dev = hidden.shape[0]
    members = mem_dev * lax.axis_size("mem")
    total = members * hidden.shape[2] * lax.axis_size("pts")
    scale = 1.0 / math.sqrt(total)
    eps_fair = 0.05 / members
    pair_coef = (1.0 - eps_fair) / (members * (members - 1))
    pre = (
        jnp.einsum("oi,mip->mop", w_first, hidden, preferred_element_type=jnp.float32)
        + b_first[None, :, None]
    )
    act = gelu_value(pre).astype(jnp.bfloat16)
    pred = jnp.einsum("vh,mhp->mvp", w_out, act, preferred_element_type=jnp.float32)
    every = lax.all_gather(pred, "mem", axis=0, tiled=True)
    pairs = pair_terms(pred, every)
    weights = area[None, None, :] * var_weight[None, :, None]
    grad_pred = (weights * (smooth_sign(pred - target[None]) / members - pair_coef * pairs)).astype(
        jnp.bfloat16
    )
    grad_act = jnp.einsum("vh,mvp->mhp", w_out, grad_pred, preferred_element_type=jnp.float32)
    grad_pre = (grad_act * gelu_slope(pre)).astype(jnp.bfloat16)
    sum_first = jnp.einsum("mop,mip->oi", grad_pre, hidden, preferred_element_type=jnp.float32)
    sum_out = jnp.einsum("mvp,mhp->vh", grad_pred, act, preferred_element_type=jnp.float32)
    sum_bias = jnp.sum(grad_pre.astype(jnp.float32), axis=(0, 2))
    sum_first, sum_out, sum_bias = lax.psum((sum_first, sum_out, sum_bias), ("mem", "pts"))
    grad_hidden = jnp.einsum(
        "oi,mop->mip", w_first, grad_pre, preferred_element_type=jnp.float32
    ).astype(jnp.bfloat16)
    return (grad_hidden, sum_first * scale, sum_out * scale, sum_bias * scale)


def solution(mesh):
    return jax.shard_map(
        per_device,
        mesh=mesh,
        in_specs=(P("mem", None, "pts"), P(), P(), P(), P(None, "pts"), P("pts"), P()),
        out_specs=(P("mem", None, "pts"), P(), P(), P()),
        check_vma=False,
    )
```

profile of v0, /device:TPU:1, one launch (start us, length us, event | category | flops | bytes accessed | tf_op | source)
XLA Modules:
  0.0 370.5 jit_solution(10977263151159686592)
XLA Ops:
  7.2 0.0 copy-start
  7.2 0.0 copy-start.6
  7.2 0.0 copy-start.9
  7.2 0.0 copy-start.8
  7.2 0.0 all-gather.2.cloned.1.call-start
  7.3 1.5 copy-done
  8.8 11.1 %multiply_convert_fusion = (bf16[2,1024,1024]{1,2,0:T(8,128)(2,1)S(1)}, f32[2,1024,1024]{2,1,0:T(8,128)}) fusion(f32[1024]{0:T(1024)} %param.9, bf16[2,1024,1024]{2,1,0:T(8,128)(2,1)} %param.7, bf16[1024,1024]{1,0:T(8,128)(2,1)S(1)} %copy-done), kind=kOutput, calls=%fused_computation.13 | convolution fusion | flops 4315938816 | bytes 18878464 | tf_op jit(solution)/shard_map/oi,mip->mop/dot_general | solution.py:40
  19.9 0.0 copy-start.1
  19.9 2.0 copy-done.1
  21.9 0.0 copy-done.6
  21.9 2.4 convolution_bitcast_fusion.1
  24.3 0.0 copy-start.3
  24.3 0.0 all-gather.2.cloned.1.call-update
  24.3 0.2 all-reduce.3.cloned.1.call-start
  24.5 0.0 copy-done.9
  24.5 0.0 copy-done.8
  24.5 0.1 broadcast_multiply_fusion.2
  24.6 40.6 %all-gather.2.cloned.1.call-done = f32[8,100,1024]{2,1,0:T(8,128)} async-done(((f32[2,100,1024]{2,1,0:T(8,128)}), f32[8,100,1024]{2,1,0:T(8,128)}) %all-gather.2.cloned.1.call-update) | async-done | bytes 3276816 | tf_op jit(solution)/shard_map/all_gather | solution.py:45
  65.2 0.0 copy-start.4
  65.3 0.0 copy-start.2
  65.3 4.0 %copy.23 = f32[8,100,1024]{2,0,1:T(8,128)S(1)} copy(f32[8,100,1024]{2,1,0:T(8,128)} %all-gather.2.cloned.1.call-done) | data formatting | bytes 6553600 | tf_op jit(solution)/shard_map/all_gather | solution.py:45
  69.3 0.0 copy-done.3
  69.3 0.0 copy-start.7
  69.3 0.0 copy-start.11
  69.3 0.0 copy-start.12
  69.3 2.7 fusion.9
  72.0 0.0 copy-done.4
  72.0 0.3 multiply_convert_fusion.1
  72.3 0.0 copy-done.2
  72.3 1.5 convolution_bitcast_fusion.2
  73.9 0.0 copy-done.7
  73.9 0.0 copy-done.11
  73.9 0.0 copy-done.12
  73.9 0.0 copy-start.10
  73.9 6.5 %convert_reduce_fusion = (f32[1024]{0:T(1024)S(1)}, bf16[2,1024,1024]{1,2,0:T(8,128)(2,1)S(1)}) fusion(f32[2,1024,1024]{2,1,0:T(8,128)S(1)} %copy-done.12, f32[1024]{0:T(1024)S(1)} %copy-done.11, bf16[2,100,1024]{2,1,0:T(8,128)(2,1)S(1)} %multiply_convert_fusion.1, bf16[100,1024]{1,0:T(8,128)(2,1)S(1)} %copy-done.7), kind=kOutput, calls=%fused_computation.12 | convolution fusion | flops 465566720 | bytes 13205504 | tf_op jit(solution)/shard_map/vh,mvp->mhp/dot_general | solution.py:51
  80.4 0.0 copy-start.13
  80.4 2.0 copy-done.13
  82.4 0.0 copy-done.10
  82.4 6.1 %convolution_bitcast_fusion = f32[1024,1024]{1,0:T(8,128)} fusion(bf16[2,1024,1024]{1,2,0:T(8,128)(2,1)S(1)} %get-tuple-element.21, bf16[2,1024,1024]{2,1,0:T(8,128)(2,1)S(1)} %copy-done.10), kind=kOutput, calls=%fused_computation.18 | convolution fusion | flops 4294967296 | bytes 12582912 | tf_op jit(solution)/shard_map/mop,mip->oi/dot_general | solution.py:53
  88.5 0.0 all-reduce.3.cloned.1.call-update
  88.6 8.3 %convert_bitcast_fusion = bf16[2,1024,1024]{1,2,0:T(8,128)(2,1)} fusion(bf16[2,1024,1024]{1,2,0:T(8,128)(2,1)} %copy-done.13, bf16[1024,1024]{1,0:T(8,128)(2,1)S(1)} %copy-done), kind=kOutput, calls=%fused_computation.17 | convolution fusion | flops 4297064448 | bytes 10485760 | tf_op jit(solution)/shard_map/oi,mop->mip/dot_general | solution.py:57
  96.8 6.2 %copy.26 = bf16[2,1024,1024]{2,1,0:T(8,128)(2,1)} copy(bf16[2,1024,1024]{1,2,0:T(8,128)(2,1)} %convert_bitcast_fusion) | data formatting | bytes 8388608
  103.0 77.3 %psum.23 = f32[1024]{0:T(1024)S(1)} all-reduce(f32[1024]{0:T(1024)S(1)} %get-tuple-element.20), channel_id=1, replica_groups=mesh['mem'=4,'pts'=64] {'mem','pts'}, use_global_device_ids=true, to_apply=%region_4.0 | all-reduce | flops 1024 | bytes 8192 | tf_op jit(solution)/shard_map/psum | solution.py:56
  180.3 0.6 broadcast_multiply_fusion.3
  180.9 176.7 %all-reduce.3.cloned.1.call-done = (f32[1024,1024]{1,0:T(8,128)}, f32[100,1024]{1,0:T(8,128)}) async-done(((f32[1024,1024]{1,0:T(8,128)}, f32[100,1024]{1,0:T(8,128)}), (f32[1024,1024]{1,0:T(8,128)}, f32[100,1024]{1,0:T(8,128)})) %all-reduce.3.cloned.1.call-update) | async-done | bytes 4603920 | tf_op jit(solution)/shard_map/psum | solution.py:56
  357.7 5.2 %broadcast_multiply_fusion = f32[1024,1024]{1,0:T(8,128)} fusion(f32[1024,1024]{1,0:T(8,128)} %get-tuple-element.16), kind=kLoop, calls=%fused_computation.22 | loop fusion | flops 1048576 | bytes 8388608 | tf_op jit(solution)/shard_map/mul | solution.py:60
  362.9 0.0 copy-done.5
  362.9 0.8 broadcast_multiply_fusion.1
  (1 shorter events, 0.0 us)
Async XLA Ops:
  7.2 1.6 copy-start
  7.2 14.7 %copy-start.6 = (bf16[100,1024]{1,0:T(8,128)(2,1)S(1)}, bf16[100,1024]{1,0:T(8,128)(2,1)}, u32[]{:S(2)}) copy-start(bf16[100,1024]{1,0:T(8,128)(2,1)} %param.10) | copy-start | bytes 614404
  7.2 17.3 %copy-start.9 = (f32[100]{0:T(128)S(1)}, f32[100]{0:T(128)}, u32[]{:S(2)}) copy-start(f32[100]{0:T(128)} %param.13) | copy-start | bytes 1204
  7.2 17.3 %copy-start.8 = (f32[1024]{0:T(1024)S(1)}, f32[1024]{0:T(1024)}, u32[]{:S(2)}) copy-start(f32[1024]{0:T(1024)} %param.12) | copy-start | bytes 12292
  7.2 58.0 %all-gather.2.cloned.1.call-start = ((), (), s32[]{:S(2)}) async-start(), calls=%async_computation | async-start | bytes 4259840 | tf_op jit(solution)/shard_map/all_gather | solution.py:45
  19.9 2.0 copy-start.1
  24.3 45.0 %copy-start.3 = (f32[2,100,1024]{2,1,0:T(8,128)S(1)}, f32[2,100,1024]{2,1,0:T(8,128)}, u32[]{:S(2)}) copy-start(f32[2,100,1024]{2,1,0:T(8,128)} %convolution_bitcast_fusion.1) | copy-start | bytes 2457604
  24.3 333.4 %all-reduce.3.cloned.1.call-start = ((), (), s32[]{:S(2)}) async-start(), calls=%async_computation.1 | async-start | bytes 9240576 | tf_op jit(solution)/shard_map/psum | solution.py:56
  65.2 6.8 %copy-start.4 = (f32[100,1024]{1,0:T(8,128)S(1)}, f32[100,1024]{1,0:T(8,128)}, u32[]{:S(2)}) copy-start(f32[100,1024]{1,0:T(8,128)} %param.11) | copy-start | bytes 1228804
  65.3 7.1 %copy-start.2 = (bf16[2,1024,1024]{1,2,0:T(8,128)(2,1)S(1)}, bf16[2,1024,1024]{1,2,0:T(8,128)(2,1)}, u32[]{:S(2)}) copy-start(bf16[2,1024,1024]{1,2,0:T(8,128)(2,1)} %copy-done.1) | copy-start | bytes 12582916
  69.3 4.6 %copy-start.7 = (bf16[100,1024]{1,0:T(8,128)(2,1)S(1)}, bf16[100,1024]{1,0:T(8,128)(2,1)}, u32[]{:S(2)}) copy-start(bf16[100,1024]{1,0:T(8,128)(2,1)} %param.10) | copy-start | bytes 614404
  69.3 4.6 %copy-start.11 = (f32[1024]{0:T(1024)S(1)}, f32[1024]{0:T(1024)}, u32[]{:S(2)}) copy-start(f32[1024]{0:T(1024)} %param.9) | copy-start | bytes 12292
  69.3 4.6 %copy-start.12 = (f32[2,1024,1024]{2,1,0:T(8,128)S(1)}, f32[2,1024,1024]{2,1,0:T(8,128)}, u32[]{:S(2)}) copy-start(f32[2,1024,1024]{2,1,0:T(8,128)} %get-tuple-element.19) | copy-start | bytes 25165828
  73.9 8.5 %copy-start.10 = (bf16[2,1024,1024]{2,1,0:T(8,128)(2,1)S(1)}, bf16[2,1024,1024]{2,1,0:T(8,128)(2,1)}, u32[]{:S(2)}) copy-start(bf16[2,1024,1024]{2,1,0:T(8,128)(2,1)} %param.7) | copy-start | bytes 12582916
  80.4 2.0 copy-start.13
  357.7 5.2 %copy-start.5 = (f32[100,1024]{1,0:T(8,128)S(1)}, f32[100,1024]{1,0:T(8,128)}, u32[]{:S(2)}) copy-start(f32[100,1024]{1,0:T(8,128)} %get-tuple-element.17) | copy-start | bytes 1228804
Sparse Core Ops, SparseCore 0:
  24.4 40.8 all-gather.1
  88.7 268.9 all-reduce.2
where the time goes:
time: 372 us; the launch traced here: 370 us
  waiting for transfers between devices  217 us (58%)
  blocking collectives  77.3 us (21%)
  matrix products  35.9 us (10%)
  local copies, waits for them, and re-layouts  15.8 us (4%)
  between operations  14.2 us (4%)
  other arithmetic  9.65 us (3%)
    psum x1, waiting for transfers between devices, per_device(): lax.psum((sum_first, sum_out, sum_bias), ('mem', 'pts'))  177 us
    psum x1, blocking collectives, per_device(): lax.psum((sum_first, sum_out, sum_bias), ('mem', 'pts'))  77.3 us
    all_gather x1, waiting for transfers between devices, per_device(): every = lax.all_gather(pred, 'mem', axis=0, tiled=True)  40.6 us
    unnamed x29, local copies, waits for them, and re-layouts  11.8 us
    dot_general x1, matrix products, per_device(): jnp.einsum('oi,mip->mop', w_first, hidden, preferred_element_type=jnp.flo...  11.1 us
    dot_general x1, matrix products, per_device(): jnp.einsum('oi,mop->mip', w_first, grad_pre, preferred_element_type=jnp.f...  8.29 us
  transfers between devices with their start and end apart: 2, of which 2 were waited for; matrix products, arithmetic and copies ran while one was open for 4% of the time, Pallas kernels for 0%

commit v1 on v0

--- a/solution.py
+++ b/solution.py
@@ -3,8 +3,12 @@
 import jax
 import jax.numpy as jnp
 from jax import lax
+from jax.experimental import pallas as pl
+from jax.experimental.pallas import tpu as pltpu
 from jax.sharding import PartitionSpec as P
 
+MESH = pl.DeviceIdType.MESH
+f32 = jnp.float32
 curve = 0.044715
 root_coef = 0.7978845608
 delta_sq = 0.0025
@@ -27,6 +31,172 @@
 
 def pair_terms(own, others):
     return jnp.sum(smooth_sign(own[:, None] - others[None]), axis=1)
+
+
+def make_ar(NC, scale):
+    pr = 32 // NC
+    half = 16 * pr
+    n = NC + 1
+
+    def kern(gw, gs, ow, os, rcw, rcs, aw, as_, r1w, r1s, b1w, b1s, r2w, r2s, zw, zs, rzw, rzs,
+             s_c, q_c, s_1, q_1, s_2, q_2, s_z, q_z, s_az, q_az, s_a2, q_a2, s_a1, q_a1, s_ac, q_ac):
+        m = lax.axis_index("mem"); p = lax.axis_index("pts")
+        c = m % 2
+        x = (m // 2) * 2 + p % 2
+        y = (p // 2) % 4
+        z = p // 8
+        def at(xx, yy, zz, cc):
+            return ((xx // 2) * 2 + cc, (zz * 4 + yy) * 2 + xx % 2)
+        def xo(d): return at((x + d) % 4, y, z, c)
+        def yo(d): return at(x, (y + d) % 4, z, c)
+        def zo(d): return at(x, y, (z + d) % 8, c)
+        other = at(x, y, z, 1 - c)
+        bar = pltpu.get_barrier_semaphore()
+        peers = [other] + [xo(d) for d in (1, 2, 3)] + [yo(d) for d in (1, 2, 3)] + [zo(d) for d in range(1, 8)]
+        for t in peers:
+            pl.semaphore_signal(bar, inc=1, device_id=t, device_id_type=MESH)
+        pl.semaphore_wait(bar, len(peers))
+        sends = []
+        def copy(src, dst, ss, rs, dev):
+            cp = pltpu.make_async_remote_copy(src_ref=src, dst_ref=dst, send_sem=ss, recv_sem=rs, device_id=dev, device_id_type=MESH)
+            cp.start(); sends.append(cp); return cp
+        def mo(v, k): return pl.multiple_of(v, k)
+
+        pend = {}
+        def core_send(k):
+            if k == 0:
+                src, dst = gs.at[:, pl.ds(mo((1 - c) * 512, 512), 512)], rcs
+            else:
+                base = (k - 1) * 2 * half
+                src, dst = gw.at[pl.ds(mo(base + (1 - c) * half, half), half)], rcw.at[k - 1]
+            pend["c", k] = copy(src, dst, s_c.at[k], q_c.at[k], other)
+        def st_core(k):
+            pend["c", k].wait_recv()
+            if k == 0:
+                as_[...] = gs[:, pl.ds(mo(c * 512, 512), 512)] + rcs[...]
+                a, r1, hw, q = as_, r1s, 256, 8
+            else:
+                base = (k - 1) * 2 * half
+                aw[k - 1] = gw[pl.ds(mo(base + c * half, half), half)] + rcw[k - 1]
+                a, r1, hw, q = aw.at[k - 1], r1w.at[k - 1], 512, pr
+            for d in (2, 1, 3):
+                xx = (x + d) % 4; yy = (y + d) % 4
+                pend[1, k, 0, d] = copy(a.at[pl.ds(mo(xx * 4 * q, 4 * q), 4 * q), pl.ds(0, hw)], r1.at[0, d - 1], s_1.at[k, 0, d - 1], q_1.at[k, 0, d - 1], xo(d))
+                pend[1, k, 1, d] = copy(a.at[pl.ds(mo(yy * 4 * q, 4 * q), 4 * q), pl.ds(hw, hw)], r1.at[1, d - 1], s_1.at[k, 1, d - 1], q_1.at[k, 1, d - 1], yo(d))
+        def st_1(k):
+            if k == 0:
+                a, r1, b1, r2, hw, q = as_, r1s, b1s, r2s, 256, 8
+            else:
+                a, r1, b1, r2, hw, q = aw.at[k - 1], r1w.at[k - 1], b1w.at[k - 1], r2w.at[k - 1], 512, pr
+            for h in (0, 1):
+                me, nxt, dv = ((x, y, yo), (y, x, xo))[h]
+                for d in (1, 2, 3):
+                    pend[1, k, h, d].wait_recv()
+                b1[h] = a[pl.ds(mo(me * 4 * q, 4 * q), 4 * q), pl.ds(h * hw, hw)] + r1[h, 0] + r1[h, 1] + r1[h, 2]
+                for d in (2, 1, 3):
+                    t = (nxt + d) % 4
+                    pend[2, k, h, d] = copy(b1.at[h, pl.ds(mo(t * q, q), q)], r2.at[h, d - 1], s_2.at[k, h, d - 1], q_2.at[k, h, d - 1], dv(d))
+        def st_2(k):
+            if k == 0:
+                b1, r2, zb, hw, q = b1s, r2s, zs, 256, 8
+            else:
+                b1, r2, zb, hw, q = b1w.at[k - 1], r2w.at[k - 1], zw.at[k - 1], 512, pr
+            for h in (0, 1):
+                nxt = (y, x)[h]
+                for d in (1, 2, 3):
+                    pend[2, k, h, d].wait_recv()
+                zb[:, pl.ds(h * hw, hw)] = b1[h, pl.ds(mo(nxt * q, q), q)] + r2[h, 0] + r2[h, 1] + r2[h, 2]
+            for d in (4, 3, 5, 2, 6, 1, 7):
+                t = (z + d) % 8
+                if k == 0:
+                    src, dst = zs, rzs.at[d - 1]
+                else:
+                    src, dst = zw.at[k - 1, :, pl.ds(mo(t * 128, 128), 128)], rzw.at[k - 1, d - 1]
+                pend["z", k, d] = copy(src, dst, s_z.at[k, d - 1], q_z.at[k, d - 1], zo(d))
+        def piece_rows(k, h, q):
+            j = (4 * x + y, 4 * y + x)[h]
+            return j * q
+        def st_z(k):
+            for d in range(1, 8):
+                pend["z", k, d].wait_recv()
+            if k == 0:
+                tot = zs[...]
+                for d in range(7):
+                    tot = tot + rzs[d]
+                tot = tot * scale
+                for h in (0, 1):
+                    os[pl.ds(mo(piece_rows(k, h, 8), 8), 8), pl.ds(mo(c * 512 + h * 256, 256), 256)] = tot[:, h * 256:(h + 1) * 256]
+                st_ag2(k)
+            else:
+                tot = zw[k - 1, :, pl.ds(mo(z * 128, 128), 128)]
+                for d in range(7):
+                    tot = tot + rzw[k - 1, d]
+                hz = z // 4
+                j = (1 - hz) * (4 * x + y) + hz * (4 * y + x)
+                row = mo((k - 1) * 2 * half + c * half + j * pr, 8)
+                dst = ow.at[pl.ds(row, pr), pl.ds(mo(z * 128, 128), 128)]
+                dst[...] = tot * scale
+                for d in (4, 3, 5, 2, 6, 1, 7):
+                    pend["az", k, d] = copy(dst, dst, s_az.at[k, d - 1], q_az.at[k, d - 1], zo(d))
+        def st_ag2(k):
+            if k > 0:
+                for d in range(1, 8):
+                    pend["az", k, d].wait_recv()
+            for h in (0, 1):
+                dv = (yo, xo)[h]
+                if k == 0:
+                    blk = os.at[pl.ds(mo(piece_rows(k, h, 8), 8), 8), pl.ds(mo(c * 512 + h * 256, 256), 256)]
+                else:
+                    blk = ow.at[pl.ds(mo((k - 1) * 2 * half + c * half + piece_rows(k, h, pr), 8), pr), pl.ds(h * 512, 512)]
+                for d in (2, 1, 3):
+                    pend["a2", k, h, d] = copy(blk, blk, s_a2.at[k, h, d - 1], q_a2.at[k, h, d - 1], dv(d))
+        def st_ag1(k):
+            for h in (0, 1):
+                for d in (1, 2, 3):
+                    pend["a2", k, h, d].wait_recv()
+                me, dv = ((x, xo), (y, yo))[h]
+                if k == 0:
+                    blk = os.at[pl.ds(mo(me * 32, 32), 32), pl.ds(mo(c * 512 + h * 256, 256), 256)]
+                else:
+                    blk = ow.at[pl.ds(mo((k - 1) * 2 * half + c * half + me * 4 * pr, 8), 4 * pr), pl.ds(h * 512, 512)]
+                for d in (2, 1, 3):
+                    pend["a1", k, h, d] = copy(blk, blk, s_a1.at[k, h, d - 1], q_a1.at[k, h, d - 1], dv(d))
+        def st_agc(k):
+            for h in (0, 1):
+                for d in (1, 2, 3):
+                    pend["a1", k, h, d].wait_recv()
+            if k == 0:
+                blk = os.at[:, pl.ds(mo(c * 512, 512), 512)]
+            else:
+                blk = ow.at[pl.ds(mo((k - 1) * 2 * half + c * half, half), half)]
+            pend["ac", k] = copy(blk, blk, s_ac.at[k], q_ac.at[k], other)
+        def nothing(k): pass
+        def st_z_ag(k): pass
+        for k in range(n):
+            core_send(k)
+        stages = [st_core, st_1, st_2, st_z, lambda k: st_ag2(k) if k else None, st_ag1, st_agc]
+        for t in range(n + len(stages) - 1):
+            for s in range(len(stages)):
+                k = t - s
+                if 0 <= k < n:
+                    stages[s](k)
+        for k in range(n):
+            pend["ac", k].wait_recv()
+        for cp in sends:
+            cp.wait_send()
+
+    V = pltpu.VMEM
+    D = pltpu.SemaphoreType.DMA
+    scratch = [V((NC, half, 1024), f32), V((128, 512), f32), V((NC, half, 1024), f32), V((128, 512), f32),
+               V((NC, 2, 3, 4 * pr, 512), f32), V((2, 3, 32, 256), f32), V((NC, 2, 4 * pr, 512), f32), V((2, 32, 256), f32),
+               V((NC, 2, 3, pr, 512), f32), V((2, 3, 8, 256), f32), V((NC, pr, 1024), f32), V((8, 512), f32),
+               V((NC, 7, pr, 128), f32), V((7, 8, 512), f32)]
+    for shp in ((n,), (n, 2, 3), (n, 2, 3), (n, 7), (n, 7), (n, 2, 3), (n, 2, 3), (n,)):
+        scratch += [D(shp), D(shp)]
+    return pl.pallas_call(kern, out_shape=(jax.ShapeDtypeStruct((1024, 1024), f32), jax.ShapeDtypeStruct((128, 1024), f32)),
+        in_specs=[pl.BlockSpec(memory_space=pltpu.VMEM)] * 2, out_specs=[pl.BlockSpec(memory_space=pltpu.VMEM)] * 2,
+        scratch_shapes=scratch, name=f"allreduce{NC}",
+        compiler_params=pltpu.CompilerParams(collective_id=10 + NC, has_side_effects=True, vmem_limit_bytes=48 * 2**20))
 
 
 def per_device(hidden, w_first, b_first, w_out, target, area, var_weight):
@@ -53,11 +223,12 @@
     sum_first = jnp.einsum("mop,mip->oi", grad_pre, hidden, preferred_element_type=jnp.float32)
     sum_out = jnp.einsum("mvp,mhp->vh", grad_pred, act, preferred_element_type=jnp.float32)
     sum_bias = jnp.sum(grad_pre.astype(jnp.float32), axis=(0, 2))
-    sum_first, sum_out, sum_bias = lax.psum((sum_first, sum_out, sum_bias), ("mem", "pts"))
+    small = jnp.concatenate([sum_out, sum_bias[None], jnp.zeros((27, 1024), f32)], axis=0)
+    sum_first, small = make_ar(4, scale)(sum_first, small)
     grad_hidden = jnp.einsum(
         "oi,mop->mip", w_first, grad_pre, preferred_element_type=jnp.float32
     ).astype(jnp.bfloat16)
-    return (grad_hidden, sum_first * scale, sum_out * scale, sum_bias * scale)
+    return (grad_hidden, sum_first, small[:100], small[100])
 
 
 def solution(mesh):

time: 372 us -> 169 us (0.45)
  waiting for transfers between devices: 217 us -> 40.8 us
  blocking collectives: 77.3 us -> 0 us
  Pallas kernels: 0 us -> 55.9 us
  other arithmetic: 9.65 us -> 3.2 us
  local copies, waits for them, and re-layouts: 15.8 us -> 21.9 us
    psum x1 -> x0, waiting for transfers between devices: 177 us -> none  [per_device(): lax.psum((sum_first, sum_out, sum_bias), ('mem', 'pts'))]
    psum x1 -> x0, blocking collectives: 77.3 us -> none  [per_device(): lax.psum((sum_first, sum_out, sum_bias), ('mem', 'pts'))]
    pallas_call x0 -> x1, Pallas kernels: none -> 55.9 us  [per_device(): sum_first, small = make_ar(4, scale)(sum_first, small)]
    mul x3 -> x0, other arithmetic: 6.57 us -> none  [per_device(): return (grad_hidden, sum_first * scale, sum_out * scale, sum_bias * scale)]
    unnamed x29 -> x28, local copies, waits for them, and re-layouts: 11.8 us -> 16.4 us
  transfers between devices with their start and end apart: 2 -> 1, of which waited for: 2 -> 1; matrix products, arithmetic and copies ran while one was open for 4% -> 0% of each run, Pallas kernels for 0% -> 0%
where the time goes in v1:
time: 169 us
  Pallas kernels  55.9 us (33%)
  waiting for transfers between devices  40.8 us (24%)
  matrix products  32.9 us (19%)
  local copies, waits for them, and re-layouts  21.9 us (13%)
  between operations  14.2 us (8%)
  other arithmetic  3.2 us (2%)
    pallas_call x1, Pallas kernels, per_device(): sum_first, small = make_ar(4, scale)(sum_first, small)  55.9 us
    all_gather x1, waiting for transfers between devices, per_device(): every = lax.all_gather(pred, 'mem', axis=0, tiled=True)  40.8 us
    unnamed x28, local copies, waits for them, and re-layouts  16.4 us
    dot_general x1, matrix products, per_device(): jnp.einsum('oi,mip->mop', w_first, hidden, preferred_element_type=jnp.flo...  11.2 us
    dot_general x1, matrix products, per_device(): jnp.einsum('vh,mvp->mhp', w_out, grad_pred, preferred_element_type=jnp.fl...  6.5 us
    dot_general x1, matrix products, per_device(): jnp.einsum('mop,mip->oi', grad_pre, hidden, preferred_element_type=jnp.fl...  6.08 us
    dot_general x1, matrix products, per_device(): jnp.einsum('oi,mop->mip', w_first, grad_pre, preferred_element_type=jnp.f...  6.01 us
    all_gather x1, local copies, waits for them, and re-layouts, per_device(): every = lax.all_gather(pred, 'mem', axis=0, tiled=True)  4.01 us
  transfers between devices with their start and end apart: 1, of which 1 were waited for; matrix products, arithmetic and copies ran while one was open for 0% of the time, Pallas kernels for 0%

profile of v1, /device:TPU:1, one launch (start us, length us, event | category | flops | bytes accessed | tf_op | source)
XLA Modules:
  0.0 168.9 jit_solution(17355182500736379995)
XLA Ops:
  7.2 0.0 copy-start
  7.2 0.0 copy-start.6
  7.2 0.0 copy-start.9
  7.2 0.0 copy-start.8
  7.2 0.0 all-gather.2.cloned.1.call-start
  7.3 1.5 copy-done
  8.8 11.2 %multiply_convert_fusion = (bf16[2,1024,1024]{1,2,0:T(8,128)(2,1)S(1)}, f32[2,1024,1024]{2,1,0:T(8,128)}) fusion(f32[1024]{0:T(1024)} %param.9, bf16[2,1024,1024]{2,1,0:T(8,128)(2,1)} %param.7, bf16[1024,1024]{1,0:T(8,128)(2,1)S(1)} %copy-done), kind=kOutput, calls=%fused_computation.13 | convolution fusion | flops 4315938816 | bytes 18878464 | tf_op jit(solution)/shard_map/oi,mip->mop/dot_general | solution.py:210
  20.0 0.0 copy-start.2
  20.0 2.0 %copy-done.2 = bf16[2,1024,1024]{1,2,0:T(8,128)(2,1)} copy-done((bf16[2,1024,1024]{1,2,0:T(8,128)(2,1)}, bf16[2,1024,1024]{1,2,0:T(8,128)(2,1)S(1)}, u32[]{:S(2)}) %copy-start.2) | copy-done | bytes 4194328
  21.9 0.0 copy-done.6
  21.9 2.4 %convolution_bitcast_fusion.1 = f32[2,100,1024]{2,1,0:T(8,128)} fusion(bf16[2,1024,1024]{1,2,0:T(8,128)(2,1)S(1)} %get-tuple-element.20, bf16[100,1024]{1,0:T(8,128)(2,1)S(1)} %copy-done.6), kind=kOutput, calls=%fused_computation.22 | convolution fusion | flops 419430400 | bytes 5218304 | tf_op jit(solution)/shard_map/vh,mhp->mvp/dot_general | solution.py:214
  24.3 0.0 copy-start.4
  24.3 0.0 all-gather.2.cloned.1.call-update
  24.3 0.1 pad.2.clone
  24.4 0.0 copy-done.9
  24.4 0.0 copy-done.8
  24.4 0.1 broadcast_multiply_fusion
  24.5 0.0 copy-start.11
  24.5 40.8 %all-gather.2.cloned.1.call-done = f32[8,100,1024]{2,1,0:T(8,128)} async-done(((f32[2,100,1024]{2,1,0:T(8,128)}), f32[8,100,1024]{2,1,0:T(8,128)}) %all-gather.2.cloned.1.call-update) | async-done | bytes 3276816 | tf_op jit(solution)/shard_map/all_gather | solution.py:215
  65.3 0.0 copy-start.5
  65.3 0.0 copy-start.7
  65.3 0.0 copy-start.12
  65.3 4.0 %copy.23 = f32[8,100,1024]{2,0,1:T(8,128)S(1)} copy(f32[8,100,1024]{2,1,0:T(8,128)} %all-gather.2.cloned.1.call-done) | data formatting | bytes 6553600 | tf_op jit(solution)/shard_map/all_gather | solution.py:215
  69.3 0.0 copy-done.4
  69.3 2.7 %fusion.9 = f32[2,100,1024]{2,1,0:T(8,128)S(1)} fusion(f32[8,100,1024]{2,0,1:T(8,128)S(1)} %copy.23, f32[2,100,1024]{2,1,0:T(8,128)S(1)} %copy-done.4), kind=kLoop, calls=%fused_computation.16 | loop fusion | flops 7987200 | bytes 4915200 | tf_op jit(solution)/shard_map/reduce_sum | solution.py:33
  72.0 0.0 copy-done.5
  72.0 0.3 multiply_convert_fusion.1
  72.3 0.0 copy-done.11
  72.3 0.0 copy-done.7
  72.4 0.0 copy-done.12
  72.4 6.5 %convert_reduce_fusion = (f32[1024]{0:T(1024)S(1)}, bf16[2,1024,1024]{1,2,0:T(8,128)(2,1)S(1)}) fusion(f32[2,1024,1024]{2,1,0:T(8,128)S(1)} %copy-done.12, f32[1024]{0:T(1024)S(1)} %copy-done.11, bf16[2,100,1024]{2,1,0:T(8,128)(2,1)S(1)} %multiply_convert_fusion.1, bf16[100,1024]{1,0:T(8,128)(2,1)S(1)} %copy-done.7), kind=kOutput, calls=%fused_computation.12 | convolution fusion | flops 465566720 | bytes 13205504 | tf_op jit(solution)/shard_map/vh,mvp->mhp/dot_general | solution.py:221
  78.9 0.0 copy-start.10
  78.9 6.0 %convert_bitcast_fusion = bf16[2,1024,1024]{1,2,0:T(8,128)(2,1)} fusion(bf16[2,1024,1024]{1,2,0:T(8,128)(2,1)S(1)} %get-tuple-element.23, bf16[1024,1024]{1,0:T(8,128)(2,1)S(1)} %copy-done), kind=kOutput, calls=%fused_computation.17 | convolution fusion | flops 4297064448 | bytes 10485760 | tf_op jit(solution)/shard_map/oi,mop->mip/dot_general | solution.py:228
  84.9 0.0 copy-done.10
  84.9 0.0 copy-start.3
  84.9 6.1 %convolution_bitcast_fusion.gw = f32[1024,1024]{1,0:T(8,128)} fusion(bf16[2,1024,1024]{1,2,0:T(8,128)(2,1)S(1)} %get-tuple-element.23, bf16[2,1024,1024]{2,1,0:T(8,128)(2,1)S(1)} %copy-done.10), kind=kOutput, calls=%fused_computation.18 | convolution fusion | flops 4294967296 | bytes 12582912 | tf_op jit(solution)/shard_map/mop,mip->oi/dot_general | solution.py:223
  91.0 0.0 copy-done.3
  91.0 0.8 convolution_bitcast_fusion.2
  91.7 0.1 maximum_maximum_fusion.gs
  91.8 55.9 %allreduce4.1 = (f32[1024,1024]{1,0:T(8,128)S(1)}, f32[128,1024]{1,0:T(8,128)S(1)}) custom-call(f32[1024,1024]{1,0:T(8,128)} %convolution_bitcast_fusion.gw, f32[128,1024]{1,0:T(8,128)S(1)} %maximum_maximum_fusion.gs), custom_call_target="tpu_custom_call" | custom-call | tf_op jit(solution)/shard_map/allreduce4/pallas_call | solution.py:227
  147.8 0.0 copy-start.1
  147.8 1.9 %copy-done.1 = f32[1024,1024]{1,0:T(8,128)} copy-done((f32[1024,1024]{1,0:T(8,128)}, f32[1024,1024]{1,0:T(8,128)S(1)}, u32[]{:S(2)}) %copy-start.1) | copy-done | bytes 4194328
  149.7 0.8 slice.6
  150.5 0.6 slice.7
  151.1 6.2 %copy.26 = bf16[2,1024,1024]{2,1,0:T(8,128)(2,1)} copy(bf16[2,1024,1024]{1,2,0:T(8,128)(2,1)} %convert_bitcast_fusion) | data formatting | bytes 8388608
  157.3 4.8 %copy.32 = f32[1024,1024]{1,0:T(8,128)} copy(f32[1024,1024]{1,0:T(8,128)} %copy-done.1) | data formatting | bytes 8388608
  (1 shorter events, 0.0 us)
Async XLA Ops:
  7.2 1.6 copy-start
  7.2 14.7 %copy-start.6 = (bf16[100,1024]{1,0:T(8,128)(2,1)S(1)}, bf16[100,1024]{1,0:T(8,128)(2,1)}, u32[]{:S(2)}) copy-start(bf16[100,1024]{1,0:T(8,128)(2,1)} %param.10) | copy-start | bytes 614404
  7.2 17.2 %copy-start.9 = (f32[100]{0:T(128)S(1)}, f32[100]{0:T(128)}, u32[]{:S(2)}) copy-start(f32[100]{0:T(128)} %param.13) | copy-start | bytes 1204
  7.2 17.2 %copy-start.8 = (f32[1024]{0:T(1024)S(1)}, f32[1024]{0:T(1024)}, u32[]{:S(2)}) copy-start(f32[1024]{0:T(1024)} %param.12) | copy-start | bytes 12292
  7.2 58.1 %all-gather.2.cloned.1.call-start = ((), (), s32[]{:S(2)}) async-start(), calls=%async_computation | async-start | bytes 4259840 | tf_op jit(solution)/shard_map/all_gather | solution.py:215
  20.0 2.0 %copy-start.2 = (bf16[2,1024,1024]{1,2,0:T(8,128)(2,1)}, bf16[2,1024,1024]{1,2,0:T(8,128)(2,1)S(1)}, u32[]{:S(2)}) copy-start(bf16[2,1024,1024]{1,2,0:T(8,128)(2,1)S(1)} %get-tuple-element.20) | copy-start | bytes 12582916
  24.3 45.0 %copy-start.4 = (f32[2,100,1024]{2,1,0:T(8,128)S(1)}, f32[2,100,1024]{2,1,0:T(8,128)}, u32[]{:S(2)}) copy-start(f32[2,100,1024]{2,1,0:T(8,128)} %convolution_bitcast_fusion.1) | copy-start | bytes 2457604
  24.5 47.8 %copy-start.11 = (f32[1024]{0:T(1024)S(1)}, f32[1024]{0:T(1024)}, u32[]{:S(2)}) copy-start(f32[1024]{0:T(1024)} %param.9) | copy-start | bytes 12292
  65.3 6.7 %copy-start.5 = (f32[100,1024]{1,0:T(8,128)S(1)}, f32[100,1024]{1,0:T(8,128)}, u32[]{:S(2)}) copy-start(f32[100,1024]{1,0:T(8,128)} %param.11) | copy-start | bytes 1228804
  65.3 7.1 %copy-start.7 = (bf16[100,1024]{1,0:T(8,128)(2,1)S(1)}, bf16[100,1024]{1,0:T(8,128)(2,1)}, u32[]{:S(2)}) copy-start(bf16[100,1024]{1,0:T(8,128)(2,1)} %param.10) | copy-start | bytes 614404
  65.3 7.1 %copy-start.12 = (f32[2,1024,1024]{2,1,0:T(8,128)S(1)}, f32[2,1024,1024]{2,1,0:T(8,128)}, u32[]{:S(2)}) copy-start(f32[2,1024,1024]{2,1,0:T(8,128)} %get-tuple-element.21) | copy-start | bytes 25165828
  78.9 6.0 %copy-start.10 = (bf16[2,1024,1024]{2,1,0:T(8,128)(2,1)S(1)}, bf16[2,1024,1024]{2,1,0:T(8,128)(2,1)}, u32[]{:S(2)}) copy-start(bf16[2,1024,1024]{2,1,0:T(8,128)(2,1)} %param.7) | copy-start | bytes 12582916
  84.9 6.1 %copy-start.3 = (bf16[2,1024,1024]{1,2,0:T(8,128)(2,1)S(1)}, bf16[2,1024,1024]{1,2,0:T(8,128)(2,1)}, u32[]{:S(2)}) copy-start(bf16[2,1024,1024]{1,2,0:T(8,128)(2,1)} %copy-done.2) | copy-start | bytes 12582916
  147.8 1.9 %copy-start.1 = (f32[1024,1024]{1,0:T(8,128)}, f32[1024,1024]{1,0:T(8,128)S(1)}, u32[]{:S(2)}) copy-start(f32[1024,1024]{1,0:T(8,128)S(1)} %get-tuple-element.29) | copy-start | bytes 12582916
Sparse Core Ops, SparseCore 0:
  24.4 40.8 all-gather.1

commit v2 on v1

--- a/solution.py
+++ b/solution.py
@@ -9,36 +9,37 @@
 
 MESH = pl.DeviceIdType.MESH
 f32 = jnp.float32
+bf16 = jnp.bfloat16
 curve = 0.044715
 root_coef = 0.7978845608
 delta_sq = 0.0025
-
-
-def gelu_value(u):
-    return 0.5 * u * (1.0 + jnp.tanh(root_coef * (u + curve * u * u * u)))
-
-
-def gelu_slope(u):
-    inner = jnp.tanh(root_coef * (u + curve * u * u * u))
-    return 0.5 * (1.0 + inner) + 0.5 * u * (1.0 - inner * inner) * root_coef * (
-        1.0 + 3.0 * curve * u * u
-    )
+NQ = 4
+CQ = 256
+NC = 4
+NT = (((1,), (1,)), ((), ()))
 
 
 def smooth_sign(d):
-    return d / jnp.sqrt(d * d + delta_sq)
-
-
-def pair_terms(own, others):
-    return jnp.sum(smooth_sign(own[:, None] - others[None]), axis=1)
-
-
-def make_ar(NC, scale):
+    return d * lax.rsqrt(d * d + delta_sq)
+
+
+def dot(a, b):
+    return jnp.dot(a, b, preferred_element_type=f32)
+
+
+def dot_nt(a, b):
+    return lax.dot_general(a, b, NT, preferred_element_type=f32)
+
+
+def make_kernel(members, pair_coef):
     pr = 32 // NC
     half = 16 * pr
     n = NC + 1
 
-    def kern(gw, gs, ow, os, rcw, rcs, aw, as_, r1w, r1s, b1w, b1s, r2w, r2s, zw, zs, rzw, rzs,
+    def kern(hid_hbm, w, bcol, wo, tgt, area, vw, gh_hbm, ow_hbm, os_hbm,
+             hid, wt, wot, act, slope, gpre, ghs, pred, pc, px, py, gpf, gp, bacc, gw, gs, ow, os,
+             rcw, rcs, aw, as_, r1w, r1s, b1w, b1s, r2w, r2s, zw, zs, rzw, rzs,
+             q_h, q_gh, q_ow, s_x, q_x, s_p, q_p, s_f, q_f,
              s_c, q_c, s_1, q_1, s_2, q_2, s_z, q_z, s_az, q_az, s_a2, q_a2, s_a1, q_a1, s_ac, q_ac):
         m = lax.axis_index("mem"); p = lax.axis_index("pts")
         c = m % 2
@@ -51,17 +52,32 @@
         def yo(d): return at(x, (y + d) % 4, z, c)
         def zo(d): return at(x, y, (z + d) % 8, c)
         other = at(x, y, z, 1 - c)
+        def mo(v, k): return pl.multiple_of(v, k)
+        def cols(q): return pl.ds(mo(q * CQ, CQ), CQ)
+
+        def load(q, i):
+            return pltpu.make_async_copy(hid_hbm.at[i, :, cols(q)], hid.at[q, :, pl.ds(i * CQ, CQ)], q_h.at[q, i])
+        def store(q, i):
+            return pltpu.make_async_copy(ghs.at[q, :, pl.ds(i * CQ, CQ)], gh_hbm.at[i, :, cols(q)], q_gh.at[q, i])
+        for q in range(NQ):
+            for i in range(2):
+                load(q, i).start()
+
         bar = pltpu.get_barrier_semaphore()
         peers = [other] + [xo(d) for d in (1, 2, 3)] + [yo(d) for d in (1, 2, 3)] + [zo(d) for d in range(1, 8)]
         for t in peers:
             pl.semaphore_signal(bar, inc=1, device_id=t, device_id_type=MESH)
-        pl.semaphore_wait(bar, len(peers))
+
+        def remote(src, dst, ss, rs, dev):
+            return pltpu.make_async_remote_copy(src_ref=src, dst_ref=dst, send_sem=ss, recv_sem=rs, device_id=dev, device_id_type=MESH)
+        def cp_x(q): return remote(pred.at[q], px.at[q], s_x.at[q], q_x.at[q], xo(2))
+        def cp_p(q): return remote(pred.at[q], pc.at[q], s_p.at[q], q_p.at[q], other)
+        def cp_f(q): return remote(px.at[q], py.at[q], s_f.at[q], q_f.at[q], other)
+
         sends = []
         def copy(src, dst, ss, rs, dev):
-            cp = pltpu.make_async_remote_copy(src_ref=src, dst_ref=dst, send_sem=ss, recv_sem=rs, device_id=dev, device_id_type=MESH)
+            cp = remote(src, dst, ss, rs, dev)
             cp.start(); sends.append(cp); return cp
-        def mo(v, k): return pl.multiple_of(v, k)
-
         pend = {}
         def core_send(k):
             if k == 0:
@@ -123,7 +139,7 @@
                 tot = zs[...]
                 for d in range(7):
                     tot = tot + rzs[d]
-                tot = tot * scale
+                tot = tot
                 for h in (0, 1):
                     os[pl.ds(mo(piece_rows(k, h, 8), 8), 8), pl.ds(mo(c * 512 + h * 256, 256), 256)] = tot[:, h * 256:(h + 1) * 256]
                 st_ag2(k)
@@ -135,7 +151,7 @@
                 j = (1 - hz) * (4 * x + y) + hz * (4 * y + x)
                 row = mo((k - 1) * 2 * half + c * half + j * pr, 8)
                 dst = ow.at[pl.ds(row, pr), pl.ds(mo(z * 128, 128), 128)]
-                dst[...] = tot * scale
+                dst[...] = tot
                 for d in (4, 3, 5, 2, 6, 1, 7):
                     pend["az", k, d] = copy(dst, dst, s_az.at[k, d - 1], q_az.at[k, d - 1], zo(d))
         def st_ag2(k):
@@ -170,65 +186,162 @@
             else:
                 blk = ow.at[pl.ds(mo((k - 1) * 2 * half + c * half, half), half)]
             pend["ac", k] = copy(blk, blk, s_ac.at[k], q_ac.at[k], other)
-        def nothing(k): pass
-        def st_z_ag(k): pass
-        for k in range(n):
+        def forward(q):
+            for i in range(2):
+                load(q, i).wait()
+            for o in range(4):
+                rows = pl.ds(o * 256, 256)
+                u = dot(w[rows, :], hid[q]) + bcol[rows, :]
+                u2 = u * u
+                t = jnp.tanh(u * (root_coef + root_coef * curve * u2))
+                h = 0.5 + 0.5 * t
+                act[q, rows, :] = (u * h).astype(bf16)
+                slope[q, rows, :] = h + (0.5 * root_coef) * u * (1.0 - t * t) * (1.0 + 3.0 * curve * u2)
+            pred[q] = dot(wo[...], act[q])[:104]
+
+        def grad_pred(q):
+            def row(r, _):
+                rr = pl.ds(mo(r * 8, 8), 8)
+                a = pred[q, rr, :]
+                s01 = smooth_sign(a[:, :CQ] - a[:, CQ:])
+                pairs = jnp.concatenate([s01, -s01], axis=1)
+                for ref in (pc, px, py):
+                    v = ref[q, rr, :]
+                    sw = jnp.concatenate([v[:, CQ:], v[:, :CQ]], axis=1)
+                    pairs = pairs + (smooth_sign(a - v) + smooth_sign(a - sw))
+                tg = tgt[rr, cols(q)]
+                wt_ = vw[rr, :] * area[:, cols(q)]
+                d = a - jnp.concatenate([tg, tg], axis=1)
+                gpf[rr, :] = jnp.concatenate([wt_, wt_], axis=1) * (smooth_sign(d) * (1.0 / members) - pair_coef * pairs)
+                return 0
+            lax.fori_loop(0, 13, row, 0)
+            gp[q] = gpf[...].astype(bf16)
+
+        def back_pre(q):
+            for o in range(4):
+                rows = pl.ds(o * 256, 256)
+                g = (dot(wot[rows, :], gp[q]) * slope[q, rows, :]).astype(bf16)
+                gpre[q, rows, :] = g
+                gf = g.astype(f32)
+                bacc[rows, :] += (gf[:, :128] + gf[:, 128:256]) + (gf[:, 256:384] + gf[:, 384:])
+            gs[:104, :] += dot_nt(gp[q], act[q])[:104]
+
+        def back_w(q, o):
+            rows = pl.ds(o * 256, 256)
+            gw[rows, :] += dot_nt(gpre[q, rows, :], hid[q])
+
+        def back_h(q):
+            for o in range(4):
+                rows = pl.ds(o * 256, 256)
+                ghs[q, rows, :] = dot(wt[rows, :], gpre[q]).astype(bf16)
+            for i in range(2):
+                store(q, i).start()
+
+        def fwd_step(q, _):
+            forward(q)
+            @pl.when(q == 0)
+            def _():
+                pl.semaphore_wait(bar, len(peers))
+            cp_x(q).start()
+            cp_p(q).start()
+            return 0
+        lax.fori_loop(0, NQ, fwd_step, 0)
+
+        gw[...] = jnp.zeros((1024, 1024), f32)
+        gs[...] = jnp.zeros((128, 1024), f32)
+        bacc[...] = jnp.zeros((1024, 128), f32)
+        gpf[...] = jnp.zeros((128, 2 * CQ), f32)
+        for i in range(4):
+            wt[pl.ds(i * 256, 256), :] = w[:, i * 256:(i + 1) * 256].T
+        wot[...] = wo[...].T
+
+        def arrive(q):
+            cp_x(q).wait_recv()
+            cp_f(q).start()
+            cp_p(q).wait_recv()
+            cp_f(q).wait_recv()
+            grad_pred(q)
+            back_pre(q)
+        def bwd_step(q, _):
+            arrive(q)
+            for o in range(4):
+                back_w(q, o)
+            back_h(q)
+            return 0
+        lax.fori_loop(0, NQ - 1, bwd_step, 0)
+        last = NQ - 1
+        arrive(last)
+        ones = jnp.ones((8, 128), f32)
+        gs[104:112, :] = lax.dot_general(ones, bacc[...], NT, precision=lax.Precision.HIGHEST, preferred_element_type=f32)
+        core_send(0)
+        for k in range(1, n):
+            back_w(last, k - 1)
             core_send(k)
-        stages = [st_core, st_1, st_2, st_z, lambda k: st_ag2(k) if k else None, st_ag1, st_agc]
+        def st_out(k):
+            pend["ac", k].wait_recv()
+            if k == 0:
+                cp = pltpu.make_async_copy(os, os_hbm, q_ow.at[0])
+            else:
+                rows = pl.ds((k - 1) * 2 * half, 2 * half)
+                cp = pltpu.make_async_copy(ow.at[rows], ow_hbm.at[rows], q_ow.at[k])
+            cp.start()
+            pend["out", k] = cp
+        stages = [st_core, st_1, st_2, st_z, lambda k: st_ag2(k) if k else None, st_ag1, st_agc, st_out]
         for t in range(n + len(stages) - 1):
             for s in range(len(stages)):
                 k = t - s
                 if 0 <= k < n:
                     stages[s](k)
+            if t == 1:
+                back_h(last)
         for k in range(n):
-            pend["ac", k].wait_recv()
+            pend["out", k].wait()
         for cp in sends:
             cp.wait_send()
+        def finish(q, _):
+            for i in range(2):
+                store(q, i).wait()
+            cp_x(q).wait_send()
+            cp_p(q).wait_send()
+            cp_f(q).wait_send()
+            return 0
+        lax.fori_loop(0, NQ, finish, 0)
 
     V = pltpu.VMEM
     D = pltpu.SemaphoreType.DMA
-    scratch = [V((NC, half, 1024), f32), V((128, 512), f32), V((NC, half, 1024), f32), V((128, 512), f32),
+    W2 = 2 * CQ
+    scratch = [V((NQ, 1024, W2), bf16), V((1024, 1024), bf16), V((1024, 128), bf16), V((NQ, 1024, W2), bf16), V((NQ, 1024, W2), f32),
+               V((NQ, 1024, W2), bf16), V((NQ, 1024, W2), bf16),
+               V((NQ, 104, W2), f32), V((NQ, 104, W2), f32), V((NQ, 104, W2), f32), V((NQ, 104, W2), f32),
+               V((128, W2), f32), V((NQ, 128, W2), bf16), V((1024, 128), f32), V((1024, 1024), f32), V((128, 1024), f32),
+               V((1024, 1024), f32), V((128, 1024), f32)]
+    scratch += [V((NC, half, 1024), f32), V((128, 512), f32), V((NC, half, 1024), f32), V((128, 512), f32),
                V((NC, 2, 3, 4 * pr, 512), f32), V((2, 3, 32, 256), f32), V((NC, 2, 4 * pr, 512), f32), V((2, 32, 256), f32),
                V((NC, 2, 3, pr, 512), f32), V((2, 3, 8, 256), f32), V((NC, pr, 1024), f32), V((8, 512), f32),
                V((NC, 7, pr, 128), f32), V((7, 8, 512), f32)]
+    scratch += [D((NQ, 2)), D((NQ, 2)), D((n,))] + [D((NQ,))] * 6
     for shp in ((n,), (n, 2, 3), (n, 2, 3), (n, 7), (n, 7), (n, 2, 3), (n, 2, 3), (n,)):
         scratch += [D(shp), D(shp)]
-    return pl.pallas_call(kern, out_shape=(jax.ShapeDtypeStruct((1024, 1024), f32), jax.ShapeDtypeStruct((128, 1024), f32)),
-        in_specs=[pl.BlockSpec(memory_space=pltpu.VMEM)] * 2, out_specs=[pl.BlockSpec(memory_space=pltpu.VMEM)] * 2,
-        scratch_shapes=scratch, name=f"allreduce{NC}",
-        compiler_params=pltpu.CompilerParams(collective_id=10 + NC, has_side_effects=True, vmem_limit_bytes=48 * 2**20))
+    vm = pl.BlockSpec(memory_space=pltpu.VMEM)
+    hbm = pl.BlockSpec(memory_space=pl.ANY)
+    return pl.pallas_call(kern,
+        out_shape=(jax.ShapeDtypeStruct((2, 1024, 1024), bf16), jax.ShapeDtypeStruct((1024, 1024), f32), jax.ShapeDtypeStruct((128, 1024), f32)),
+        in_specs=[hbm, vm, vm, vm, vm, vm, vm], out_specs=[hbm, hbm, hbm],
+        scratch_shapes=scratch, name="fused",
+        compiler_params=pltpu.CompilerParams(collective_id=3, has_side_effects=True, vmem_limit_bytes=60 * 2**20))
 
 
 def per_device(hidden, w_first, b_first, w_out, target, area, var_weight):
-    mem_dev = hidden.shape[0]
-    members = mem_dev * lax.axis_size("mem")
+    members = hidden.shape[0] * lax.axis_size("mem")
     total = members * hidden.shape[2] * lax.axis_size("pts")
     scale = 1.0 / math.sqrt(total)
     eps_fair = 0.05 / members
     pair_coef = (1.0 - eps_fair) / (members * (members - 1))
-    pre = (
-        jnp.einsum("oi,mip->mop", w_first, hidden, preferred_element_type=jnp.float32)
-        + b_first[None, :, None]
-    )
-    act = gelu_value(pre).astype(jnp.bfloat16)
-    pred = jnp.einsum("vh,mhp->mvp", w_out, act, preferred_element_type=jnp.float32)
-    every = lax.all_gather(pred, "mem", axis=0, tiled=True)
-    pairs = pair_terms(pred, every)
-    weights = area[None, None, :] * var_weight[None, :, None]
-    grad_pred = (weights * (smooth_sign(pred - target[None]) / members - pair_coef * pairs)).astype(
-        jnp.bfloat16
-    )
-    grad_act = jnp.einsum("vh,mvp->mhp", w_out, grad_pred, preferred_element_type=jnp.float32)
-    grad_pre = (grad_act * gelu_slope(pre)).astype(jnp.bfloat16)
-    sum_first = jnp.einsum("mop,mip->oi", grad_pre, hidden, preferred_element_type=jnp.float32)
-    sum_out = jnp.einsum("mvp,mhp->vh", grad_pred, act, preferred_element_type=jnp.float32)
-    sum_bias = jnp.sum(grad_pre.astype(jnp.float32), axis=(0, 2))
-    small = jnp.concatenate([sum_out, sum_bias[None], jnp.zeros((27, 1024), f32)], axis=0)
-    sum_first, small = make_ar(4, scale)(sum_first, small)
-    grad_hidden = jnp.einsum(
-        "oi,mop->mip", w_first, grad_pre, preferred_element_type=jnp.float32
-    ).astype(jnp.bfloat16)
-    return (grad_hidden, sum_first, small[:100], small[100])
+    wo = jnp.pad(w_out, ((0, 28), (0, 0)))
+    tgt = jnp.pad(target, ((0, 4), (0, 0)))
+    vw = jnp.pad(var_weight, (0, 4))[:, None]
+    grad_hidden, ow, os = make_kernel(members, pair_coef)(hidden, w_first, b_first[:, None], wo, tgt, area[None], vw)
+    return (grad_hidden, ow * scale, os[:100] * scale, os[104] * scale)
 
 
 def solution(mesh):

time: 169 us -> 107 us (0.63)
  waiting for transfers between devices: 40.8 us -> 0 us
  Pallas kernels: 55.9 us -> 89.3 us
  matrix products: 32.9 us -> 0 us
  between operations: 14.2 us -> 0.64 us
  local copies, waits for them, and re-layouts: 21.9 us -> 8.56 us
  other arithmetic: 3.2 us -> 8.43 us
    all_gather x1 -> x0, waiting for transfers between devices: 40.8 us -> none  [per_device(): every = lax.all_gather(pred, 'mem', axis=0, tiled=True)]
    pallas_call x1, Pallas kernels: 55.9 us -> 89.3 us  [per_device(): make_kernel(members, pair_coef)]
    dot_general x6 -> x0, matrix products: 32.9 us -> none  [the longest x1 11.2 us: per_device(): jnp.einsum('oi,mip->mop', w_first, hidden, preferred_element_type=jnp.flo...]
    unnamed x28 -> x3, local copies, waits for them, and re-layouts: 16.4 us -> 2.02 us
    mul x1 -> x3, other arithmetic: 0.09 us -> 8.43 us  [per_device(): return (grad_hidden, ow * scale, os[:100] * scale, os[104] * scale)]
    all_gather x1 -> x0, local copies, waits for them, and re-layouts: 4.01 us -> none  [per_device(): every = lax.all_gather(pred, 'mem', axis=0, tiled=True)]
    pad x0 -> x2, local copies, waits for them, and re-layouts: none -> 3.45 us  [the longest x1 1.79 us: per_device(): tgt = jnp.pad(target, ((0, 4), (0, 0)))]
    broadcast_in_dim x1 -> x3, local copies, waits for them, and re-layouts: 0.01 us -> 3.09 us  [the longest x1 1.71 us: per_device(): b_first[:, None]]
  transfers between devices with their start and end apart: 1 -> 0, of which waited for: 1 -> 0; matrix products, arithmetic and copies ran while one was open for 0% -> 0% of each run, Pallas kernels for 0% -> 0%
where the time goes in v2:
time: 107 us
  Pallas kernels  89.3 us (83%)
  local copies, waits for them, and re-layouts  8.56 us (8%)
  other arithmetic  8.43 us (8%)
    pallas_call x1, Pallas kernels, per_device(): make_kernel(members, pair_coef)  89.3 us
    mul x3, other arithmetic, per_device(): return (grad_hidden, ow * scale, os[:100] * scale, os[104] * scale)  8.43 us

profile of v2, /device:TPU:1, one launch (start us, length us, event | category | flops | bytes accessed | tf_op | source)
XLA Modules:
  0.0 106.9 jit_solution(12818846609344175688)
XLA Ops:
  0.6 1.7 %copy.12.bcol = f32[1024,1]{1,0:T(8,128)} copy(f32[1024,1]{0,1:T(1,128)} %bitcast.5) | data formatting | bytes 8192 | tf_op jit(solution)/shard_map/broadcast_in_dim | solution.py:343
  2.3 1.8 %pad.13.tgt = f32[104,1024]{1,0:T(8,128)} pad(f32[100,1024]{1,0:T(8,128)} %param.11, f32[]{:T(128)} %constant.2.clone.1), padding=0_4x0_0 | pad | bytes 835588 | tf_op jit(solution)/shard_map/jit(_pad)/pad | solution.py:341
  4.1 1.7 %pad.12.wo = bf16[128,1024]{1,0:T(8,128)(2,1)} pad(bf16[100,1024]{1,0:T(8,128)(2,1)} %param.10, bf16[]{:T(256)} %constant.3.clone.1), padding=0_28x0_0 | pad | bytes 466946 | tf_op jit(solution)/shard_map/jit(_pad)/pad | solution.py:340
  5.8 0.7 pad_bitcast_fusion
  6.5 0.7 copy.13.vw
  7.2 89.3 %fused.1 = (bf16[2,1024,1024]{2,1,0:T(8,128)(2,1)}, f32[1024,1024]{1,0:T(8,128)}, f32[128,1024]{1,0:T(8,128)}) custom-call(bf16[2,1024,1024]{2,1,0:T(8,128)(2,1)} %hid_hbm.1, bf16[1024,1024]{1,0:T(8,128)(2,1)} %w.1, f32[1024,1]{1,0:T(8,128)} %copy.12.bcol, bf16[128,1024]{1,0:T(8,128)(2,1)} %pad.12.wo, f32[104,1024]{1,0:T(8,128)} %pad.13.tgt, ...), custom_call_target="tpu_custom_call" | custom-call | tf_op jit(solution)/shard_map/fused/pallas_call | solution.py:343
  96.5 1.8 %slice_multiply_fusion = f32[100,1024]{1,0:T(8,128)} fusion(f32[128,1024]{1,0:T(8,128)} %get-tuple-element.9), kind=kLoop, calls=%fused_computation.1 | loop fusion | flops 102400 | bytes 819200 | tf_op jit(solution)/shard_map/mul | solution.py:344
  98.3 1.4 %slice_multiply_fusion.1 = f32[1,1024]{1,0:T(1,128)} fusion(f32[128,1024]{1,0:T(8,128)} %get-tuple-element.9), kind=kLoop, calls=%fused_computation.2 | loop fusion | flops 1024 | bytes 8192 | tf_op jit(solution)/shard_map/mul | solution.py:344
  99.7 0.0 copy-start
  99.7 5.3 %broadcast_multiply_fusion = f32[1024,1024]{1,0:T(8,128)} fusion(f32[1024,1024]{1,0:T(8,128)} %get-tuple-element.8), kind=kLoop, calls=%fused_computation | loop fusion | flops 1048576 | bytes 8388608 | tf_op jit(solution)/shard_map/mul | solution.py:344
  104.9 0.0 copy-done
  104.9 2.0 %copy.15 = bf16[2,1024,1024]{2,1,0:T(8,128)(2,1)} copy(bf16[2,1024,1024]{2,1,0:T(8,128)(2,1)S(1)} %copy-done) | data formatting | bytes 8388608
Async XLA Ops:
  99.7 5.3 %copy-start = (bf16[2,1024,1024]{2,1,0:T(8,128)(2,1)S(1)}, bf16[2,1024,1024]{2,1,0:T(8,128)(2,1)}, u32[]{:S(2)}) copy-start(bf16[2,1024,1024]{2,1,0:T(8,128)(2,1)} %get-tuple-element.14) | copy-start | bytes 12582916

commit v3 on v2

--- a/solution.py
+++ b/solution.py
@@ -17,6 +17,13 @@
 CQ = 256
 NC = 4
 NT = (((1,), (1,)), ((), ()))
+ORDER = (
+    (0, 0), (0, 1), (1, 0), (9, 0), (9, 1), (9, 2), (9, 3), (0, 2), (1, 1), (2, 0), (9, 4), (9, 5), (9, 6), (9, 7),
+    (0, 3), (1, 2), (2, 1), (3, 0), (9, 8), (9, 9), (9, 10), (9, 11), (0, 4), (1, 3), (2, 2), (3, 1), (4, 0),
+    (9, 12), (9, 13), (9, 14), (9, 15), (1, 4), (2, 3), (3, 2), (4, 1), (5, 0), (9, 16), (9, 17), (9, 18), (9, 19),
+    (2, 4), (3, 3), (4, 2), (5, 1), (6, 0), (3, 4), (4, 3), (5, 2), (6, 1), (7, 0), (4, 4), (5, 3), (6, 2), (7, 1),
+    (5, 4), (6, 3), (7, 2), (6, 4), (7, 3), (7, 4),
+)
 
 
 def smooth_sign(d):
@@ -31,15 +38,15 @@
     return lax.dot_general(a, b, NT, preferred_element_type=f32)
 
 
-def make_kernel(members, pair_coef):
+def make_kernel(members, pair_coef, scale):
     pr = 32 // NC
     half = 16 * pr
     n = NC + 1
 
-    def kern(hid_hbm, w, bcol, wo, tgt, area, vw, gh_hbm, ow_hbm, os_hbm,
-             hid, wt, wot, act, slope, gpre, ghs, pred, pc, px, py, gpf, gp, bacc, gw, gs, ow, os,
-             rcw, rcs, aw, as_, r1w, r1s, b1w, b1s, r2w, r2s, zw, zs, rzw, rzs,
-             q_h, q_gh, q_ow, s_x, q_x, s_p, q_p, s_f, q_f,
+    def kern(hid_hbm, w, brow, wo_in, tgt_in, area, vwrow, ghs, ow, os,
+             hid, wo, wot, bcol, vw, tgt, act, slope, pred, pc, px, py, gp, bacc, gw, gs,
+             rcw, rcs, as_, r1w, r1s, b1w, b1s, r2w, r2s, zw, zs, rzw, rzs,
+             q_h, s_x, q_x, s_p, q_p, s_f, q_f,
              s_c, q_c, s_1, q_1, s_2, q_2, s_z, q_z, s_az, q_az, s_a2, q_a2, s_a1, q_a1, s_ac, q_ac):
         m = lax.axis_index("mem"); p = lax.axis_index("pts")
         c = m % 2
@@ -57,8 +64,6 @@
 
         def load(q, i):
             return pltpu.make_async_copy(hid_hbm.at[i, :, cols(q)], hid.at[q, :, pl.ds(i * CQ, CQ)], q_h.at[q, i])
-        def store(q, i):
-            return pltpu.make_async_copy(ghs.at[q, :, pl.ds(i * CQ, CQ)], gh_hbm.at[i, :, cols(q)], q_gh.at[q, i])
         for q in range(NQ):
             for i in range(2):
                 load(q, i).start()
@@ -93,8 +98,9 @@
                 a, r1, hw, q = as_, r1s, 256, 8
             else:
                 base = (k - 1) * 2 * half
-                aw[k - 1] = gw[pl.ds(mo(base + c * half, half), half)] + rcw[k - 1]
-                a, r1, hw, q = aw.at[k - 1], r1w.at[k - 1], 512, pr
+                mine = gw.at[pl.ds(mo(base + c * half, half), half)]
+                mine[...] += rcw[k - 1]
+                a, r1, hw, q = mine, r1w.at[k - 1], 512, pr
             for d in (2, 1, 3):
                 xx = (x + d) % 4; yy = (y + d) % 4
                 pend[1, k, 0, d] = copy(a.at[pl.ds(mo(xx * 4 * q, 4 * q), 4 * q), pl.ds(0, hw)], r1.at[0, d - 1], s_1.at[k, 0, d - 1], q_1.at[k, 0, d - 1], xo(d))
@@ -103,7 +109,8 @@
             if k == 0:
                 a, r1, b1, r2, hw, q = as_, r1s, b1s, r2s, 256, 8
             else:
-                a, r1, b1, r2, hw, q = aw.at[k - 1], r1w.at[k - 1], b1w.at[k - 1], r2w.at[k - 1], 512, pr
+                base = (k - 1) * 2 * half
+                a, r1, b1, r2, hw, q = gw.at[pl.ds(mo(base + c * half, half), half)], r1w.at[k - 1], b1w.at[k - 1], r2w.at[k - 1], 512, pr
             for h in (0, 1):
                 me, nxt, dv = ((x, y, yo), (y, x, xo))[h]
                 for d in (1, 2, 3):
@@ -139,10 +146,10 @@
                 tot = zs[...]
                 for d in range(7):
                     tot = tot + rzs[d]
+                tot = tot * scale
                 tot = tot
                 for h in (0, 1):
                     os[pl.ds(mo(piece_rows(k, h, 8), 8), 8), pl.ds(mo(c * 512 + h * 256, 256), 256)] = tot[:, h * 256:(h + 1) * 256]
-                st_ag2(k)
             else:
                 tot = zw[k - 1, :, pl.ds(mo(z * 128, 128), 128)]
                 for d in range(7):
@@ -151,7 +158,7 @@
                 j = (1 - hz) * (4 * x + y) + hz * (4 * y + x)
                 row = mo((k - 1) * 2 * half + c * half + j * pr, 8)
                 dst = ow.at[pl.ds(row, pr), pl.ds(mo(z * 128, 128), 128)]
-                dst[...] = tot
+                dst[...] = tot * scale
                 for d in (4, 3, 5, 2, 6, 1, 7):
                     pend["az", k, d] = copy(dst, dst, s_az.at[k, d - 1], q_az.at[k, d - 1], zo(d))
         def st_ag2(k):
@@ -191,51 +198,67 @@
                 load(q, i).wait()
             for o in range(4):
                 rows = pl.ds(o * 256, 256)
-                u = dot(w[rows, :], hid[q]) + bcol[rows, :]
+                bias = bcol[rows, :]
+                u = dot(w[rows, :], hid[q]) + jnp.concatenate([bias] * 4, axis=1)
                 u2 = u * u
                 t = jnp.tanh(u * (root_coef + root_coef * curve * u2))
                 h = 0.5 + 0.5 * t
-                act[q, rows, :] = (u * h).astype(bf16)
-                slope[q, rows, :] = h + (0.5 * root_coef) * u * (1.0 - t * t) * (1.0 + 3.0 * curve * u2)
+                a = u * h
+                act[q, rows, :] = a.astype(bf16)
+                slope[q, rows, :] = h + (a - a * h) * (2.0 * root_coef + 6.0 * root_coef * curve * u2)
             pred[q] = dot(wo[...], act[q])[:104]
 
         def grad_pred(q):
-            def row(r, _):
-                rr = pl.ds(mo(r * 8, 8), 8)
-                a = pred[q, rr, :]
-                s01 = smooth_sign(a[:, :CQ] - a[:, CQ:])
-                pairs = jnp.concatenate([s01, -s01], axis=1)
-                for ref in (pc, px, py):
-                    v = ref[q, rr, :]
-                    sw = jnp.concatenate([v[:, CQ:], v[:, :CQ]], axis=1)
-                    pairs = pairs + (smooth_sign(a - v) + smooth_sign(a - sw))
-                tg = tgt[rr, cols(q)]
-                wt_ = vw[rr, :] * area[:, cols(q)]
-                d = a - jnp.concatenate([tg, tg], axis=1)
-                gpf[rr, :] = jnp.concatenate([wt_, wt_], axis=1) * (smooth_sign(d) * (1.0 / members) - pair_coef * pairs)
-                return 0
-            lax.fori_loop(0, 13, row, 0)
-            gp[q] = gpf[...].astype(bf16)
+            a = pred[q]
+            s01 = smooth_sign(a[:, :CQ] - a[:, CQ:])
+            pairs = jnp.concatenate([s01, -s01], axis=1)
+            for ref in (pc, px, py):
+                v = ref[q]
+                sw = jnp.concatenate([v[:, CQ:], v[:, :CQ]], axis=1)
+                pairs = pairs + (smooth_sign(a - v) + smooth_sign(a - sw))
+            tg = tgt[:, cols(q)]
+            va = vw[:104, :]
+            ar = area[:, cols(q)]
+            wts = jnp.concatenate([va] * 4, axis=1) * jnp.concatenate([ar, ar], axis=1)
+            d = a - jnp.concatenate([tg, tg], axis=1)
+            g = wts * (smooth_sign(d) * (1.0 / members) - pair_coef * pairs)
+            gp[q] = jnp.concatenate([g, jnp.zeros((24, 2 * CQ), f32)], axis=0).astype(bf16)
 
         def back_pre(q):
+            gs[:104, :] += dot_nt(gp[q], act[q])[:104]
             for o in range(4):
                 rows = pl.ds(o * 256, 256)
                 g = (dot(wot[rows, :], gp[q]) * slope[q, rows, :]).astype(bf16)
-                gpre[q, rows, :] = g
+                act[q, rows, :] = g
                 gf = g.astype(f32)
                 bacc[rows, :] += (gf[:, :128] + gf[:, 128:256]) + (gf[:, 256:384] + gf[:, 384:])
-            gs[:104, :] += dot_nt(gp[q], act[q])[:104]
 
         def back_w(q, o):
             rows = pl.ds(o * 256, 256)
-            gw[rows, :] += dot_nt(gpre[q, rows, :], hid[q])
-
-        def back_h(q):
-            for o in range(4):
-                rows = pl.ds(o * 256, 256)
-                ghs[q, rows, :] = dot(wt[rows, :], gpre[q]).astype(bf16)
-            for i in range(2):
-                store(q, i).start()
+            gw[rows, :] += dot_nt(act[q, rows, :], hid[q])
+
+        def late(j):
+            if j < 4:
+                for i in range(2):
+                    hid[i, pl.ds(j * 256, 256), :] = w[i * 512:(i + 1) * 512, j * 256:(j + 1) * 256].T
+            else:
+                q = (j - 4) // 4
+                rows = pl.ds((j - 4) % 4 * 256, 256)
+                ghs[q, rows, :] = (dot(hid[0, rows, :], act[q, :512, :]) + dot(hid[1, rows, :], act[q, 512:, :])).astype(bf16)
+
+        bcol[...] = jnp.broadcast_to(brow[...], (128, 1024)).T
+        vw[...] = jnp.zeros((128, 128), f32)
+        vw[:, :100] = jnp.broadcast_to(vwrow[...], (128, 100))
+        vw[...] = vw[...].T
+        tgt[96:104, :] = jnp.zeros((8, 1024), f32)
+        tgt[:100, :] = tgt_in[...]
+        gs[...] = jnp.zeros((128, 1024), f32)
+        gs[:100, :] = wo_in[...].astype(f32)
+        wo[...] = gs[...].astype(bf16)
+        wot[...] = gs[...].T.astype(bf16)
+        gs[...] = jnp.zeros((128, 1024), f32)
+        gw[...] = jnp.zeros((1024, 1024), f32)
+        bacc[...] = jnp.zeros((1024, 128), f32)
 
         def fwd_step(q, _):
             forward(q)
@@ -246,14 +269,6 @@
             cp_p(q).start()
             return 0
         lax.fori_loop(0, NQ, fwd_step, 0)
-
-        gw[...] = jnp.zeros((1024, 1024), f32)
-        gs[...] = jnp.zeros((128, 1024), f32)
-        bacc[...] = jnp.zeros((1024, 128), f32)
-        gpf[...] = jnp.zeros((128, 2 * CQ), f32)
-        for i in range(4):
-            wt[pl.ds(i * 256, 256), :] = w[:, i * 256:(i + 1) * 256].T
-        wot[...] = wo[...].T
 
         def arrive(q):
             cp_x(q).wait_recv()
@@ -266,7 +281,6 @@
             arrive(q)
             for o in range(4):
                 back_w(q, o)
-            back_h(q)
             return 0
         lax.fori_loop(0, NQ - 1, bwd_step, 0)
         last = NQ - 1
@@ -279,28 +293,15 @@
             core_send(k)
         def st_out(k):
             pend["ac", k].wait_recv()
-            if k == 0:
-                cp = pltpu.make_async_copy(os, os_hbm, q_ow.at[0])
-            else:
-                rows = pl.ds((k - 1) * 2 * half, 2 * half)
-                cp = pltpu.make_async_copy(ow.at[rows], ow_hbm.at[rows], q_ow.at[k])
-            cp.start()
-            pend["out", k] = cp
-        stages = [st_core, st_1, st_2, st_z, lambda k: st_ag2(k) if k else None, st_ag1, st_agc, st_out]
-        for t in range(n + len(stages) - 1):
-            for s in range(len(stages)):
-                k = t - s
-                if 0 <= k < n:
-                    stages[s](k)
-            if t == 1:
-                back_h(last)
-        for k in range(n):
-            pend["out", k].wait()
+        steps = {0: st_core, 1: st_1, 2: st_2, 3: st_z, 4: st_ag2, 5: st_ag1, 6: st_agc, 7: st_out}
+        for stage, k in ORDER:
+            if stage == 9:
+                late(k)
+            else:
+                steps[stage](k)
         for cp in sends:
             cp.wait_send()
         def finish(q, _):
-            for i in range(2):
-                store(q, i).wait()
             cp_x(q).wait_send()
             cp_p(q).wait_send()
             cp_f(q).wait_send()
@@ -310,25 +311,45 @@
     V = pltpu.VMEM
     D = pltpu.SemaphoreType.DMA
     W2 = 2 * CQ
-    scratch = [V((NQ, 1024, W2), bf16), V((1024, 1024), bf16), V((1024, 128), bf16), V((NQ, 1024, W2), bf16), V((NQ, 1024, W2), f32),
-               V((NQ, 1024, W2), bf16), V((NQ, 1024, W2), bf16),
+    scratch = [V((NQ, 1024, W2), bf16), V((128, 1024), bf16), V((1024, 128), bf16),
+               V((1024, 128), f32), V((128, 128), f32), V((104, 1024), f32),
+               V((NQ, 1024, W2), bf16), V((NQ, 1024, W2), f32),
                V((NQ, 104, W2), f32), V((NQ, 104, W2), f32), V((NQ, 104, W2), f32), V((NQ, 104, W2), f32),
-               V((128, W2), f32), V((NQ, 128, W2), bf16), V((1024, 128), f32), V((1024, 1024), f32), V((128, 1024), f32),
-               V((1024, 1024), f32), V((128, 1024), f32)]
-    scratch += [V((NC, half, 1024), f32), V((128, 512), f32), V((NC, half, 1024), f32), V((128, 512), f32),
+               V((NQ, 128, W2), bf16), V((1024, 128), f32), V((1024, 1024), f32), V((128, 1024), f32)]
+    scratch += [V((NC, half, 1024), f32), V((128, 512), f32), V((128, 512), f32),
                V((NC, 2, 3, 4 * pr, 512), f32), V((2, 3, 32, 256), f32), V((NC, 2, 4 * pr, 512), f32), V((2, 32, 256), f32),
                V((NC, 2, 3, pr, 512), f32), V((2, 3, 8, 256), f32), V((NC, pr, 1024), f32), V((8, 512), f32),
                V((NC, 7, pr, 128), f32), V((7, 8, 512), f32)]
-    scratch += [D((NQ, 2)), D((NQ, 2)), D((n,))] + [D((NQ,))] * 6
+    scratch += [D((NQ, 2))] + [D((NQ,))] * 6
     for shp in ((n,), (n, 2, 3), (n, 2, 3), (n, 7), (n, 7), (n, 2, 3), (n, 2, 3), (n,)):
         scratch += [D(shp), D(shp)]
     vm = pl.BlockSpec(memory_space=pltpu.VMEM)
     hbm = pl.BlockSpec(memory_space=pl.ANY)
     return pl.pallas_call(kern,
-        out_shape=(jax.ShapeDtypeStruct((2, 1024, 1024), bf16), jax.ShapeDtypeStruct((1024, 1024), f32), jax.ShapeDtypeStruct((128, 1024), f32)),
-        in_specs=[hbm, vm, vm, vm, vm, vm, vm], out_specs=[hbm, hbm, hbm],
+        out_shape=(jax.ShapeDtypeStruct((NQ, 1024, W2), bf16), jax.ShapeDtypeStruct((1024, 1024), f32), jax.ShapeDtypeStruct((128, 1024), f32)),
+        in_specs=[hbm, vm, vm, vm, vm, vm, vm], out_specs=[vm, vm, vm],
         scratch_shapes=scratch, name="fused",
-        compiler_params=pltpu.CompilerParams(collective_id=3, has_side_effects=True, vmem_limit_bytes=60 * 2**20))
+        compiler_params=pltpu.CompilerParams(collective_id=3, has_side_effects=True, vmem_limit_bytes=41 * 2**20))
+
+
+def place(ghs, ow, os):
+    def kern(ghs, ow, os, gh, gw, go, gb, out, sem):
+        out[...] = os[:100, :]
+        cps = [pltpu.make_async_copy(ow, gw, sem.at[0]), pltpu.make_async_copy(out, go, sem.at[1])]
+        for q in range(NQ):
+            for i in range(2):
+                cps.append(pltpu.make_async_copy(ghs.at[q, :, pl.ds(i * CQ, CQ)], gh.at[i, :, pl.ds(q * CQ, CQ)], sem.at[2 + 2 * q + i]))
+        for cp in cps:
+            cp.start()
+        gb[...] = os[104:105, :]
+        for cp in cps:
+            cp.wait()
+    vm = pl.BlockSpec(memory_space=pltpu.VMEM)
+    hbm = pl.BlockSpec(memory_space=pl.ANY)
+    return pl.pallas_call(kern, out_shape=(jax.ShapeDtypeStruct((2, 1024, 1024), bf16), jax.ShapeDtypeStruct((1024, 1024), f32),
+                                           jax.ShapeDtypeStruct((100, 1024), f32), jax.ShapeDtypeStruct((1, 1024), f32)),
+        in_specs=[vm, vm, vm], out_specs=[hbm, hbm, hbm, vm], scratch_shapes=[pltpu.VMEM((100, 1024), f32), pltpu.SemaphoreType.DMA((2 + 2 * NQ,))], name="place",
+        compiler_params=pltpu.CompilerParams(has_side_effects=True, vmem_limit_bytes=2**20))(ghs, ow, os)
 
 
 def per_device(hidden, w_first, b_first, w_out, target, area, var_weight):
@@ -337,11 +358,9 @@
     scale = 1.0 / math.sqrt(total)
     eps_fair = 0.05 / members
     pair_coef = (1.0 - eps_fair) / (members * (members - 1))
-    wo = jnp.pad(w_out, ((0, 28), (0, 0)))
-    tgt = jnp.pad(target, ((0, 4), (0, 0)))
-    vw = jnp.pad(var_weight, (0, 4))[:, None]
-    grad_hidden, ow, os = make_kernel(members, pair_coef)(hidden, w_first, b_first[:, None], wo, tgt, area[None], vw)
-    return (grad_hidden, ow * scale, os[:100] * scale, os[104] * scale)
+    ghs, ow, os = make_kernel(members, pair_coef, scale)(hidden, w_first, b_first[None], w_out, target, area[None], var_weight[None])
+    grad_hidden, grad_first, grad_out, grad_bias = place(ghs, ow, os)
+    return (grad_hidden, grad_first, grad_out, grad_bias[0])
 
 
 def solution(mesh):

time: 107 us -> 95.3 us (0.89)
  other arithmetic: 8.43 us -> 0 us
  local copies, waits for them, and re-layouts: 8.56 us -> 5.55 us
    mul x3 -> x0, other arithmetic: 8.43 us -> none  [per_device(): return (grad_hidden, ow * scale, os[:100] * scale, os[104] * scale)]
    unnamed x3 -> x12, local copies, waits for them, and re-layouts: 2.02 us -> 5.55 us
    pad x2 -> x0, local copies, waits for them, and re-layouts: 3.45 us -> none  [the longest x1 1.79 us: per_device(): tgt = jnp.pad(target, ((0, 4), (0, 0)))]
    broadcast_in_dim x3 -> x0, local copies, waits for them, and re-layouts: 3.09 us -> none  [the longest x1 1.71 us: per_device(): b_first[:, None]]
    pallas_call x1 -> x2, Pallas kernels: 89.3 us -> 88.8 us  [the longest x1 84.7 us: per_device(): make_kernel(members, pair_coef, scale)]
where the time goes in v3:
time: 95.3 us; the launch traced here: 95 us
  Pallas kernels  88.8 us (93%)
  local copies, waits for them, and re-layouts  5.55 us (6%)
    pallas_call x1, Pallas kernels, per_device(): make_kernel(members, pair_coef, scale)  84.7 us
    unnamed x12, local copies, waits for them, and re-layouts  5.55 us
    pallas_call x1, Pallas kernels, place(): pl.pallas_call(kern, out_shape=(jax.ShapeDtypeStruct((2, 1024, 1024), bf1...  4.09 us

profile of v3, /device:TPU:1, one launch (start us, length us, event | category | flops | bytes accessed | tf_op | source)
XLA Modules:
  0.0 95.0 jit_solution(2692242165469801622)
XLA Ops:
  0.6 0.0 copy-start
  0.6 1.6 %copy-done = bf16[1024,1024]{1,0:T(8,128)(2,1)S(1)} copy-done((bf16[1024,1024]{1,0:T(8,128)(2,1)S(1)}, bf16[1024,1024]{1,0:T(8,128)(2,1)}, u32[]{:S(2)}) %copy-start) | copy-done | bytes 2097176
  2.2 0.0 copy-start.1
  2.2 1.0 %copy-done.1 = f32[100,1024]{1,0:T(8,128)S(1)} copy-done((f32[100,1024]{1,0:T(8,128)S(1)}, f32[100,1024]{1,0:T(8,128)}, u32[]{:S(2)}) %copy-start.1) | copy-done | bytes 409624
  3.2 0.0 copy-start.2
  3.2 0.9 copy-done.2
  4.2 0.0 copy-start.3
  4.2 0.7 copy-done.3
  4.9 0.0 copy-start.4
  4.9 0.7 copy-done.4
  5.5 0.0 copy-start.5
  5.5 0.7 copy-done.5
  6.2 84.7 %fused.1 = (bf16[4,1024,512]{2,1,0:T(8,128)(2,1)S(1)}, f32[1024,1024]{1,0:T(8,128)S(1)}, f32[128,1024]{1,0:T(8,128)S(1)}) custom-call(bf16[2,1024,1024]{2,1,0:T(8,128)(2,1)} %hid_hbm.1, bf16[1024,1024]{1,0:T(8,128)(2,1)S(1)} %copy-done, f32[1,1024]{1,0:T(1,128)S(1)} %bitcast.4, bf16[100,1024]{1,0:T(8,128)(2,1)S(1)} %copy-done.2, f32[100,1024]{1,0:T(8,128)S(1)} %copy-done.1, ...), custom_call_target="tpu_custom_call" | custom-call | tf_op jit(solution)/shard_map/fused/pallas_call | solution.py:361
  91.0 4.1 %place.1 = (bf16[2,1024,1024]{2,1,0:T(8,128)(2,1)}, f32[1024,1024]{1,0:T(8,128)}, f32[100,1024]{1,0:T(8,128)}, f32[1,1024]{1,0:T(1,128)}) custom-call(bf16[4,1024,512]{2,1,0:T(8,128)(2,1)S(1)} %get-tuple-element.11.ghs, f32[1024,1024]{1,0:T(8,128)S(1)} %get-tuple-element.12.ow, f32[128,1024]{1,0:T(8,128)S(1)} %get-tuple-element.13.os), custom_call_target="tpu_custom_call" | custom-call | tf_op jit(solution)/shard_map/place/pallas_call | solution.py:349
Async XLA Ops:
  0.6 1.6 %copy-start = (bf16[1024,1024]{1,0:T(8,128)(2,1)S(1)}, bf16[1024,1024]{1,0:T(8,128)(2,1)}, u32[]{:S(2)}) copy-start(bf16[1024,1024]{1,0:T(8,128)(2,1)} %w.1) | copy-start | bytes 6291460
  2.2 1.0 %copy-start.1 = (f32[100,1024]{1,0:T(8,128)S(1)}, f32[100,1024]{1,0:T(8,128)}, u32[]{:S(2)}) copy-start(f32[100,1024]{1,0:T(8,128)} %tgt_in.1) | copy-start | bytes 1228804
  3.2 0.9 copy-start.2
  4.2 0.7 copy-start.3
  4.9 0.7 copy-start.4
  5.5 0.7 copy-start.5

commit v4 on v3

--- a/solution.py
+++ b/solution.py
@@ -13,8 +13,8 @@
 curve = 0.044715
 root_coef = 0.7978845608
 delta_sq = 0.0025
-NQ = 4
-CQ = 256
+NQ = 8
+CQ = 128
 NC = 4
 NT = (((1,), (1,)), ((), ()))
 ORDER = (
@@ -43,10 +43,10 @@
     half = 16 * pr
     n = NC + 1
 
-    def kern(hid_hbm, w, brow, wo_in, tgt_in, area, vwrow, ghs, ow, os,
-             hid, wo, wot, bcol, vw, tgt, act, slope, pred, pc, px, py, gp, bacc, gw, gs,
+    def kern(hid_hbm, w_hbm, b_hbm, wo_hbm, tgt_hbm, area_hbm, vw_hbm, ghs, ow, os,
+             w, brow, wo_in, tgt_in, area, vwrow, hid, wo, wot, bcol, vw, tgt, act, slope, pred, pc, px, py, gp, bacc, gw, gs,
              rcw, rcs, as_, r1w, r1s, b1w, b1s, r2w, r2s, zw, zs, rzw, rzs,
-             q_h, s_x, q_x, s_p, q_p, s_f, q_f,
+             q_h, q_in, s_x, q_x, s_p, q_p, s_f, q_f,
              s_c, q_c, s_1, q_1, s_2, q_2, s_z, q_z, s_az, q_az, s_a2, q_a2, s_a1, q_a1, s_ac, q_ac):
         m = lax.axis_index("mem"); p = lax.axis_index("pts")
         c = m % 2
@@ -64,6 +64,10 @@
 
         def load(q, i):
             return pltpu.make_async_copy(hid_hbm.at[i, :, cols(q)], hid.at[q, :, pl.ds(i * CQ, CQ)], q_h.at[q, i])
+        small_in = [pltpu.make_async_copy(a, b, q_in.at[i]) for i, (a, b) in enumerate(
+            ((b_hbm, brow), (vw_hbm, vwrow), (wo_hbm, wo_in), (tgt_hbm, tgt_in), (area_hbm, area), (w_hbm, w)))]
+        for cp in small_in:
+            cp.start()
         for q in range(NQ):
             for i in range(2):
                 load(q, i).start()
@@ -199,7 +203,7 @@
             for o in range(4):
                 rows = pl.ds(o * 256, 256)
                 bias = bcol[rows, :]
-                u = dot(w[rows, :], hid[q]) + jnp.concatenate([bias] * 4, axis=1)
+                u = dot(w[rows, :], hid[q]) + jnp.concatenate([bias, bias], axis=1)
                 u2 = u * u
                 t = jnp.tanh(u * (root_coef + root_coef * curve * u2))
                 h = 0.5 + 0.5 * t
@@ -219,7 +223,7 @@
             tg = tgt[:, cols(q)]
             va = vw[:104, :]
             ar = area[:, cols(q)]
-            wts = jnp.concatenate([va] * 4, axis=1) * jnp.concatenate([ar, ar], axis=1)
+            wts = jnp.concatenate([va, va], axis=1) * jnp.concatenate([ar, ar], axis=1)
             d = a - jnp.concatenate([tg, tg], axis=1)
             g = wts * (smooth_sign(d) * (1.0 / members) - pair_coef * pairs)
             gp[q] = jnp.concatenate([g, jnp.zeros((24, 2 * CQ), f32)], axis=0).astype(bf16)
@@ -231,7 +235,7 @@
                 g = (dot(wot[rows, :], gp[q]) * slope[q, rows, :]).astype(bf16)
                 act[q, rows, :] = g
                 gf = g.astype(f32)
-                bacc[rows, :] += (gf[:, :128] + gf[:, 128:256]) + (gf[:, 256:384] + gf[:, 384:])
+                bacc[rows, :] += gf[:, :128] + gf[:, 128:]
 
         def back_w(q, o):
             rows = pl.ds(o * 256, 256)
@@ -239,13 +243,19 @@
 
         def late(j):
             if j < 4:
+                for i in range(4):
+                    hid[i, pl.ds(j * 256, 256), :] = w[i * 256:(i + 1) * 256, j * 256:(j + 1) * 256].T
+            else:
+                q = (j - 4) // 2
+                rows = pl.ds((j - 4) % 2 * 512, 512)
+                g = sum(dot(hid[i, rows, :], act[q, i * 256:(i + 1) * 256, :]) for i in range(4)).astype(bf16)
                 for i in range(2):
-                    hid[i, pl.ds(j * 256, 256), :] = w[i * 512:(i + 1) * 512, j * 256:(j + 1) * 256].T
-            else:
-                q = (j - 4) // 4
-                rows = pl.ds((j - 4) % 4 * 256, 256)
-                ghs[q, rows, :] = (dot(hid[0, rows, :], act[q, :512, :]) + dot(hid[1, rows, :], act[q, 512:, :])).astype(bf16)
-
+                    ghs[i, rows, pl.ds(q * CQ, CQ)] = g[:, i * CQ:(i + 1) * CQ]
+
+        gw[...] = jnp.zeros((1024, 1024), f32)
+        bacc[...] = jnp.zeros((1024, 128), f32)
+        for cp in small_in[:5]:
+            cp.wait()
         bcol[...] = jnp.broadcast_to(brow[...], (128, 1024)).T
         vw[...] = jnp.zeros((128, 128), f32)
         vw[:, :100] = jnp.broadcast_to(vwrow[...], (128, 100))
@@ -257,8 +267,7 @@
         wo[...] = gs[...].astype(bf16)
         wot[...] = gs[...].T.astype(bf16)
         gs[...] = jnp.zeros((128, 1024), f32)
-        gw[...] = jnp.zeros((1024, 1024), f32)
-        bacc[...] = jnp.zeros((1024, 128), f32)
+        small_in[5].wait()
 
         def fwd_step(q, _):
             forward(q)
@@ -270,25 +279,30 @@
             return 0
         lax.fori_loop(0, NQ, fwd_step, 0)
 
-        def arrive(q):
+        def hand_on(q):
             cp_x(q).wait_recv()
             cp_f(q).start()
+        def arrive(q):
             cp_p(q).wait_recv()
             cp_f(q).wait_recv()
             grad_pred(q)
             back_pre(q)
         def bwd_step(q, _):
             arrive(q)
+            hand_on(q + 1)
             for o in range(4):
                 back_w(q, o)
             return 0
+        hand_on(0)
         lax.fori_loop(0, NQ - 1, bwd_step, 0)
         last = NQ - 1
         arrive(last)
+        back_w(last, 0)
+        core_send(1)
         ones = jnp.ones((8, 128), f32)
         gs[104:112, :] = lax.dot_general(ones, bacc[...], NT, precision=lax.Precision.HIGHEST, preferred_element_type=f32)
         core_send(0)
-        for k in range(1, n):
+        for k in range(2, n):
             back_w(last, k - 1)
             core_send(k)
         def st_out(k):
@@ -311,7 +325,8 @@
     V = pltpu.VMEM
     D = pltpu.SemaphoreType.DMA
     W2 = 2 * CQ
-    scratch = [V((NQ, 1024, W2), bf16), V((128, 1024), bf16), V((1024, 128), bf16),
+    scratch = [V((1024, 1024), bf16), V((1, 1024), f32), V((100, 1024), bf16), V((100, 1024), f32), V((1, 1024), f32), V((1, 100), f32),
+               V((NQ, 1024, W2), bf16), V((128, 1024), bf16), V((1024, 128), bf16),
                V((1024, 128), f32), V((128, 128), f32), V((104, 1024), f32),
                V((NQ, 1024, W2), bf16), V((NQ, 1024, W2), f32),
                V((NQ, 104, W2), f32), V((NQ, 104, W2), f32), V((NQ, 104, W2), f32), V((NQ, 104, W2), f32),
@@ -320,25 +335,22 @@
                V((NC, 2, 3, 4 * pr, 512), f32), V((2, 3, 32, 256), f32), V((NC, 2, 4 * pr, 512), f32), V((2, 32, 256), f32),
                V((NC, 2, 3, pr, 512), f32), V((2, 3, 8, 256), f32), V((NC, pr, 1024), f32), V((8, 512), f32),
                V((NC, 7, pr, 128), f32), V((7, 8, 512), f32)]
-    scratch += [D((NQ, 2))] + [D((NQ,))] * 6
+    scratch += [D((NQ, 2)), D((6,))] + [D((NQ,))] * 6
     for shp in ((n,), (n, 2, 3), (n, 2, 3), (n, 7), (n, 7), (n, 2, 3), (n, 2, 3), (n,)):
         scratch += [D(shp), D(shp)]
     vm = pl.BlockSpec(memory_space=pltpu.VMEM)
     hbm = pl.BlockSpec(memory_space=pl.ANY)
     return pl.pallas_call(kern,
-        out_shape=(jax.ShapeDtypeStruct((NQ, 1024, W2), bf16), jax.ShapeDtypeStruct((1024, 1024), f32), jax.ShapeDtypeStruct((128, 1024), f32)),
-        in_specs=[hbm, vm, vm, vm, vm, vm, vm], out_specs=[vm, vm, vm],
+        out_shape=(jax.ShapeDtypeStruct((2, 1024, 1024), bf16), jax.ShapeDtypeStruct((1024, 1024), f32), jax.ShapeDtypeStruct((128, 1024), f32)),
+        in_specs=[pl.BlockSpec(memory_space=pltpu.HBM)] * 7, out_specs=[vm, vm, vm],
         scratch_shapes=scratch, name="fused",
-        compiler_params=pltpu.CompilerParams(collective_id=3, has_side_effects=True, vmem_limit_bytes=41 * 2**20))
+        compiler_params=pltpu.CompilerParams(collective_id=3, has_side_effects=True, vmem_limit_bytes=44 * 2**20))
 
 
 def place(ghs, ow, os):
     def kern(ghs, ow, os, gh, gw, go, gb, out, sem):
         out[...] = os[:100, :]
-        cps = [pltpu.make_async_copy(ow, gw, sem.at[0]), pltpu.make_async_copy(out, go, sem.at[1])]
-        for q in range(NQ):
-            for i in range(2):
-                cps.append(pltpu.make_async_copy(ghs.at[q, :, pl.ds(i * CQ, CQ)], gh.at[i, :, pl.ds(q * CQ, CQ)], sem.at[2 + 2 * q + i]))
+        cps = [pltpu.make_async_copy(ow, gw, sem.at[0]), pltpu.make_async_copy(out, go, sem.at[1]), pltpu.make_async_copy(ghs, gh, sem.at[2])]
         for cp in cps:
             cp.start()
         gb[...] = os[104:105, :]
@@ -348,7 +360,7 @@
     hbm = pl.BlockSpec(memory_space=pl.ANY)
     return pl.pallas_call(kern, out_shape=(jax.ShapeDtypeStruct((2, 1024, 1024), bf16), jax.ShapeDtypeStruct((1024, 1024), f32),
                                            jax.ShapeDtypeStruct((100, 1024), f32), jax.ShapeDtypeStruct((1, 1024), f32)),
-        in_specs=[vm, vm, vm], out_specs=[hbm, hbm, hbm, vm], scratch_shapes=[pltpu.VMEM((100, 1024), f32), pltpu.SemaphoreType.DMA((2 + 2 * NQ,))], name="place",
+        in_specs=[vm, vm, vm], out_specs=[hbm, hbm, hbm, vm], scratch_shapes=[pltpu.VMEM((100, 1024), f32), pltpu.SemaphoreType.DMA((3,))], name="place",
         compiler_params=pltpu.CompilerParams(has_side_effects=True, vmem_limit_bytes=2**20))(ghs, ow, os)
 
 
@@ -358,7 +370,8 @@
     scale = 1.0 / math.sqrt(total)
     eps_fair = 0.05 / members
     pair_coef = (1.0 - eps_fair) / (members * (members - 1))
-    ghs, ow, os = make_kernel(members, pair_coef, scale)(hidden, w_first, b_first[None], w_out, target, area[None], var_weight[None])
+    args = [pltpu.with_memory_space_constraint(a, pltpu.HBM) for a in (hidden, w_first, b_first[None], w_out, target, area[None], var_weight[None])]
+    ghs, ow, os = make_kernel(members, pair_coef, scale)(*args)
     grad_hidden, grad_first, grad_out, grad_bias = place(ghs, ow, os)
     return (grad_hidden, grad_first, grad_out, grad_bias[0])
 

time: 95.3 us -> 91.1 us (0.956)
  local copies, waits for them, and re-layouts: 5.55 us -> 0 us
  Pallas kernels: 88.8 us -> 90.4 us
    unnamed x12 -> x0, local copies, waits for them, and re-layouts: 5.55 us -> none
    pallas_call x1, Pallas kernels: 84.7 us -> 86.2 us  [per_device(): ghs, ow, os = make_kernel(members, pair_coef, scale)(*args)]
where the time goes in v4:
time: 91.1 us; the launch traced here: 91 us
  Pallas kernels  90.4 us (99%)
    pallas_call x1, Pallas kernels, per_device(): ghs, ow, os = make_kernel(members, pair_coef, scale)(*args)  86.2 us
    pallas_call x1, Pallas kernels, place(): pl.pallas_call(kern, out_shape=(jax.ShapeDtypeStruct((2, 1024, 1024), bf1...  4.14 us

profile of v4, /device:TPU:1, one launch (start us, length us, event | category | flops | bytes accessed | tf_op | source)
XLA Modules:
  0.0 91.0 jit_solution(7682483153003234637)
XLA Ops:
  0.6 86.2 %fused.1 = (bf16[2,1024,1024]{2,1,0:T(8,128)(2,1)S(1)}, f32[1024,1024]{1,0:T(8,128)S(1)}, f32[128,1024]{1,0:T(8,128)S(1)}) custom-call(bf16[2,1024,1024]{2,1,0:T(8,128)(2,1)} %hid_hbm.1, bf16[1024,1024]{1,0:T(8,128)(2,1)} %w_hbm.1, f32[1,1024]{1,0:T(1,128)} %bitcast.4, bf16[100,1024]{1,0:T(8,128)(2,1)} %wo_hbm.1, f32[100,1024]{1,0:T(8,128)} %tgt_hbm.1, ...), custom_call_target="tpu_custom_call" | custom-call | tf_op jit(solution)/shard_map/fused/pallas_call | solution.py:374
  86.9 4.1 %place.1 = (bf16[2,1024,1024]{2,1,0:T(8,128)(2,1)}, f32[1024,1024]{1,0:T(8,128)}, f32[100,1024]{1,0:T(8,128)}, f32[1,1024]{1,0:T(1,128)}) custom-call(bf16[2,1024,1024]{2,1,0:T(8,128)(2,1)S(1)} %get-tuple-element.11.ghs, f32[1024,1024]{1,0:T(8,128)S(1)} %get-tuple-element.12.ow, f32[128,1024]{1,0:T(8,128)S(1)} %get-tuple-element.13.os), custom_call_target="tpu_custom_call" | custom-call | tf_op jit(solution)/shard_map/place/pallas_call | solution.py:361

commit v5 on v4

--- a/solution.py
+++ b/solution.py
@@ -18,11 +18,11 @@
 NC = 4
 NT = (((1,), (1,)), ((), ()))
 ORDER = (
-    (0, 0), (0, 1), (1, 0), (9, 0), (9, 1), (9, 2), (9, 3), (0, 2), (1, 1), (2, 0), (9, 4), (9, 5), (9, 6), (9, 7),
-    (0, 3), (1, 2), (2, 1), (3, 0), (9, 8), (9, 9), (9, 10), (9, 11), (0, 4), (1, 3), (2, 2), (3, 1), (4, 0),
-    (9, 12), (9, 13), (9, 14), (9, 15), (1, 4), (2, 3), (3, 2), (4, 1), (5, 0), (9, 16), (9, 17), (9, 18), (9, 19),
-    (2, 4), (3, 3), (4, 2), (5, 1), (6, 0), (3, 4), (4, 3), (5, 2), (6, 1), (7, 0), (4, 4), (5, 3), (6, 2), (7, 1),
-    (5, 4), (6, 3), (7, 2), (6, 4), (7, 3), (7, 4),
+    (0, 1), (0, 0), (0, 2), (1, 1), (9, 0), (9, 1), (9, 2), (9, 3), (0, 3), (1, 2), (2, 1), (1, 0), (9, 4), (9, 5),
+    (9, 6), (9, 7), (0, 4), (1, 3), (2, 2), (3, 1), (2, 0), (9, 8), (9, 9), (9, 10), (9, 11), (1, 4), (2, 3), (3, 2),
+    (4, 1), (9, 12), (9, 13), (9, 14), (9, 15), (2, 4), (3, 3), (4, 2), (5, 1), (3, 0), (9, 16), (9, 17), (9, 18),
+    (9, 19), (3, 4), (4, 3), (5, 2), (6, 1), (4, 0), (4, 4), (5, 3), (6, 2), (7, 1), (5, 0), (5, 4), (6, 3), (7, 2),
+    (6, 4), (7, 3), (6, 0), (7, 4),
 )
 
 
@@ -45,9 +45,10 @@
 
     def kern(hid_hbm, w_hbm, b_hbm, wo_hbm, tgt_hbm, area_hbm, vw_hbm, ghs, ow, os,
              w, brow, wo_in, tgt_in, area, vwrow, hid, wo, wot, bcol, vw, tgt, act, slope, pred, pc, px, py, gp, bacc, gw, gs,
-             rcw, rcs, as_, r1w, r1s, b1w, b1s, r2w, r2s, zw, zs, rzw, rzs,
+             rcw, rcs, as_, r1w, b1w, r2w, zw, rzw, rzs, zs, rxs, rys,
              q_h, q_in, s_x, q_x, s_p, q_p, s_f, q_f,
-             s_c, q_c, s_1, q_1, s_2, q_2, s_z, q_z, s_az, q_az, s_a2, q_a2, s_a1, q_a1, s_ac, q_ac):
+             s_c, q_c, s_1, q_1, s_2, q_2, s_z, q_z, s_az, q_az, s_a2, q_a2, s_a1, q_a1, s_ac, q_ac,
+             s_sz, q_sz, s_sx, q_sx, s_sy, q_sy, s_tx, q_tx, s_tz, q_tz):
         m = lax.axis_index("mem"); p = lax.axis_index("pts")
         c = m % 2
         x = (m // 2) * 2 + p % 2
@@ -88,115 +89,123 @@
             cp = remote(src, dst, ss, rs, dev)
             cp.start(); sends.append(cp); return cp
         pend = {}
+        def small_cols(j, w): return pl.ds(mo(c * 512 + j * w, w), w)
+        def mine(k): return gw.at[pl.ds(mo((k - 1) * 2 * half + c * half, half), half)]
+        def done(k): return ow.at[pl.ds(mo((k - 1) * 2 * half + c * half, half), half)]
+        def axis(h): return ((x, xo), (y, yo))[h]
+
         def core_send(k):
             if k == 0:
                 src, dst = gs.at[:, pl.ds(mo((1 - c) * 512, 512), 512)], rcs
             else:
-                base = (k - 1) * 2 * half
-                src, dst = gw.at[pl.ds(mo(base + (1 - c) * half, half), half)], rcw.at[k - 1]
+                src, dst = gw.at[pl.ds(mo((k - 1) * 2 * half + (1 - c) * half, half), half)], rcw.at[k - 1]
             pend["c", k] = copy(src, dst, s_c.at[k], q_c.at[k], other)
+
+        def small_0():
+            pend["c", 0].wait_recv()
+            as_[...] = gs[:, pl.ds(mo(c * 512, 512), 512)] + rcs[...]
+            for d in (4, 3, 5, 2, 6, 1, 7):
+                t = (z + d) % 8
+                pend["sz", d] = copy(as_.at[pl.ds(mo(t * 16, 16), 16)], rzs.at[d - 1], s_sz.at[d - 1], q_sz.at[d - 1], zo(d))
+        def small_1():
+            for d in range(1, 8):
+                pend["sz", d].wait_recv()
+            tot = as_[pl.ds(mo(z * 16, 16), 16), :]
+            for d in range(7):
+                tot = tot + rzs[d]
+            zs[...] = tot
+            for d in (2, 1, 3):
+                t = (x + d) % 4
+                pend["sx", d] = copy(zs.at[:, pl.ds(mo(t * 128, 128), 128)], rxs.at[d - 1], s_sx.at[d - 1], q_sx.at[d - 1], xo(d))
+        def small_2():
+            for d in range(1, 4):
+                pend["sx", d].wait_recv()
+            rys[y] = zs[:, pl.ds(mo(x * 128, 128), 128)] + rxs[0] + rxs[1] + rxs[2]
+            for d in (2, 1, 3):
+                pend["sy", d] = copy(rys.at[y], rys.at[y], s_sy.at[d - 1], q_sy.at[d - 1], yo(d))
+        def small_3():
+            for d in range(1, 4):
+                pend["sy", d].wait_recv()
+            blk = os.at[pl.ds(mo(z * 16, 16), 16), small_cols(x, 128)]
+            blk[...] = ((rys[0] + rys[1]) + (rys[2] + rys[3])) * scale
+            for d in (2, 1, 3):
+                pend["tx", d] = copy(blk, blk, s_tx.at[d - 1], q_tx.at[d - 1], xo(d))
+        def small_4():
+            for d in range(1, 4):
+                pend["tx", d].wait_recv()
+            blk = os.at[pl.ds(mo(z * 16, 16), 16), small_cols(0, 512)]
+            for d in (4, 3, 5, 2, 6, 1, 7):
+                pend["tz", d] = copy(blk, blk, s_tz.at[d - 1], q_tz.at[d - 1], zo(d))
+        def small_5():
+            for d in range(1, 8):
+                pend["tz", d].wait_recv()
+            blk = os.at[:, small_cols(0, 512)]
+            pend["ac", 0] = copy(blk, blk, s_ac.at[0], q_ac.at[0], other)
+
         def st_core(k):
             pend["c", k].wait_recv()
-            if k == 0:
-                as_[...] = gs[:, pl.ds(mo(c * 512, 512), 512)] + rcs[...]
-                a, r1, hw, q = as_, r1s, 256, 8
-            else:
-                base = (k - 1) * 2 * half
-                mine = gw.at[pl.ds(mo(base + c * half, half), half)]
-                mine[...] += rcw[k - 1]
-                a, r1, hw, q = mine, r1w.at[k - 1], 512, pr
+            a = mine(k)
+            a[...] += rcw[k - 1]
             for d in (2, 1, 3):
-                xx = (x + d) % 4; yy = (y + d) % 4
-                pend[1, k, 0, d] = copy(a.at[pl.ds(mo(xx * 4 * q, 4 * q), 4 * q), pl.ds(0, hw)], r1.at[0, d - 1], s_1.at[k, 0, d - 1], q_1.at[k, 0, d - 1], xo(d))
-                pend[1, k, 1, d] = copy(a.at[pl.ds(mo(yy * 4 * q, 4 * q), 4 * q), pl.ds(hw, hw)], r1.at[1, d - 1], s_1.at[k, 1, d - 1], q_1.at[k, 1, d - 1], yo(d))
+                for h in (0, 1):
+                    me, to = axis(h)
+                    t = (me + d) % 4
+                    pend[1, k, h, d] = copy(a.at[pl.ds(mo(t * 4 * pr, 4 * pr), 4 * pr), pl.ds(h * 512, 512)], r1w.at[k - 1, h, d - 1], s_1.at[k, h, d - 1], q_1.at[k, h, d - 1], to(d))
         def st_1(k):
-            if k == 0:
-                a, r1, b1, r2, hw, q = as_, r1s, b1s, r2s, 256, 8
-            else:
-                base = (k - 1) * 2 * half
-                a, r1, b1, r2, hw, q = gw.at[pl.ds(mo(base + c * half, half), half)], r1w.at[k - 1], b1w.at[k - 1], r2w.at[k - 1], 512, pr
-            for h in (0, 1):
-                me, nxt, dv = ((x, y, yo), (y, x, xo))[h]
+            for h in (0, 1):
+                me, to = axis(h)
+                nxt, along = axis(1 - h)
                 for d in (1, 2, 3):
                     pend[1, k, h, d].wait_recv()
-                b1[h] = a[pl.ds(mo(me * 4 * q, 4 * q), 4 * q), pl.ds(h * hw, hw)] + r1[h, 0] + r1[h, 1] + r1[h, 2]
+                b1w[k - 1, h] = mine(k)[pl.ds(mo(me * 4 * pr, 4 * pr), 4 * pr), pl.ds(h * 512, 512)] + r1w[k - 1, h, 0] + r1w[k - 1, h, 1] + r1w[k - 1, h, 2]
                 for d in (2, 1, 3):
                     t = (nxt + d) % 4
-                    pend[2, k, h, d] = copy(b1.at[h, pl.ds(mo(t * q, q), q)], r2.at[h, d - 1], s_2.at[k, h, d - 1], q_2.at[k, h, d - 1], dv(d))
+                    pend[2, k, h, d] = copy(b1w.at[k - 1, h, pl.ds(mo(t * pr, pr), pr)], r2w.at[k - 1, h, d - 1], s_2.at[k, h, d - 1], q_2.at[k, h, d - 1], along(d))
         def st_2(k):
-            if k == 0:
-                b1, r2, zb, hw, q = b1s, r2s, zs, 256, 8
-            else:
-                b1, r2, zb, hw, q = b1w.at[k - 1], r2w.at[k - 1], zw.at[k - 1], 512, pr
-            for h in (0, 1):
-                nxt = (y, x)[h]
+            for h in (0, 1):
+                nxt, along = axis(1 - h)
                 for d in (1, 2, 3):
                     pend[2, k, h, d].wait_recv()
-                zb[:, pl.ds(h * hw, hw)] = b1[h, pl.ds(mo(nxt * q, q), q)] + r2[h, 0] + r2[h, 1] + r2[h, 2]
+                zw[k - 1, :, pl.ds(h * 512, 512)] = b1w[k - 1, h, pl.ds(mo(nxt * pr, pr), pr)] + r2w[k - 1, h, 0] + r2w[k - 1, h, 1] + r2w[k - 1, h, 2]
             for d in (4, 3, 5, 2, 6, 1, 7):
                 t = (z + d) % 8
-                if k == 0:
-                    src, dst = zs, rzs.at[d - 1]
-                else:
-                    src, dst = zw.at[k - 1, :, pl.ds(mo(t * 128, 128), 128)], rzw.at[k - 1, d - 1]
-                pend["z", k, d] = copy(src, dst, s_z.at[k, d - 1], q_z.at[k, d - 1], zo(d))
-        def piece_rows(k, h, q):
-            j = (4 * x + y, 4 * y + x)[h]
-            return j * q
+                pend["z", k, d] = copy(zw.at[k - 1, :, pl.ds(mo(t * 128, 128), 128)], rzw.at[k - 1, d - 1], s_z.at[k, d - 1], q_z.at[k, d - 1], zo(d))
         def st_z(k):
             for d in range(1, 8):
                 pend["z", k, d].wait_recv()
-            if k == 0:
-                tot = zs[...]
-                for d in range(7):
-                    tot = tot + rzs[d]
-                tot = tot * scale
-                tot = tot
-                for h in (0, 1):
-                    os[pl.ds(mo(piece_rows(k, h, 8), 8), 8), pl.ds(mo(c * 512 + h * 256, 256), 256)] = tot[:, h * 256:(h + 1) * 256]
-            else:
-                tot = zw[k - 1, :, pl.ds(mo(z * 128, 128), 128)]
-                for d in range(7):
-                    tot = tot + rzw[k - 1, d]
-                hz = z // 4
-                j = (1 - hz) * (4 * x + y) + hz * (4 * y + x)
-                row = mo((k - 1) * 2 * half + c * half + j * pr, 8)
-                dst = ow.at[pl.ds(row, pr), pl.ds(mo(z * 128, 128), 128)]
-                dst[...] = tot * scale
-                for d in (4, 3, 5, 2, 6, 1, 7):
-                    pend["az", k, d] = copy(dst, dst, s_az.at[k, d - 1], q_az.at[k, d - 1], zo(d))
+            tot = zw[k - 1, :, pl.ds(mo(z * 128, 128), 128)]
+            for d in range(7):
+                tot = tot + rzw[k - 1, d]
+            hz = z // 4
+            j = (1 - hz) * (4 * x + y) + hz * (4 * y + x)
+            dst = done(k).at[pl.ds(mo(j * pr, pr), pr), pl.ds(mo(z * 128, 128), 128)]
+            dst[...] = tot * scale
+            for d in (4, 3, 5, 2, 6, 1, 7):
+                pend["az", k, d] = copy(dst, dst, s_az.at[k, d - 1], q_az.at[k, d - 1], zo(d))
         def st_ag2(k):
-            if k > 0:
-                for d in range(1, 8):
-                    pend["az", k, d].wait_recv()
-            for h in (0, 1):
-                dv = (yo, xo)[h]
-                if k == 0:
-                    blk = os.at[pl.ds(mo(piece_rows(k, h, 8), 8), 8), pl.ds(mo(c * 512 + h * 256, 256), 256)]
-                else:
-                    blk = ow.at[pl.ds(mo((k - 1) * 2 * half + c * half + piece_rows(k, h, pr), 8), pr), pl.ds(h * 512, 512)]
+            for d in range(1, 8):
+                pend["az", k, d].wait_recv()
+            for h in (0, 1):
+                me, to = axis(h)
+                nxt, along = axis(1 - h)
+                blk = done(k).at[pl.ds(mo((4 * me + nxt) * pr, pr), pr), pl.ds(h * 512, 512)]
                 for d in (2, 1, 3):
-                    pend["a2", k, h, d] = copy(blk, blk, s_a2.at[k, h, d - 1], q_a2.at[k, h, d - 1], dv(d))
+                    pend["a2", k, h, d] = copy(blk, blk, s_a2.at[k, h, d - 1], q_a2.at[k, h, d - 1], along(d))
         def st_ag1(k):
             for h in (0, 1):
+                me, to = axis(h)
                 for d in (1, 2, 3):
                     pend["a2", k, h, d].wait_recv()
-                me, dv = ((x, xo), (y, yo))[h]
-                if k == 0:
-                    blk = os.at[pl.ds(mo(me * 32, 32), 32), pl.ds(mo(c * 512 + h * 256, 256), 256)]
-                else:
-                    blk = ow.at[pl.ds(mo((k - 1) * 2 * half + c * half + me * 4 * pr, 8), 4 * pr), pl.ds(h * 512, 512)]
+                blk = done(k).at[pl.ds(mo(me * 4 * pr, 4 * pr), 4 * pr), pl.ds(h * 512, 512)]
                 for d in (2, 1, 3):
-                    pend["a1", k, h, d] = copy(blk, blk, s_a1.at[k, h, d - 1], q_a1.at[k, h, d - 1], dv(d))
+                    pend["a1", k, h, d] = copy(blk, blk, s_a1.at[k, h, d - 1], q_a1.at[k, h, d - 1], to(d))
         def st_agc(k):
             for h in (0, 1):
                 for d in (1, 2, 3):
                     pend["a1", k, h, d].wait_recv()
-            if k == 0:
-                blk = os.at[:, pl.ds(mo(c * 512, 512), 512)]
-            else:
-                blk = ow.at[pl.ds(mo((k - 1) * 2 * half + c * half, half), half)]
+            blk = done(k)
             pend["ac", k] = copy(blk, blk, s_ac.at[k], q_ac.at[k], other)
+
         def forward(q):
             for i in range(2):
                 load(q, i).wait()
@@ -299,20 +308,24 @@
         arrive(last)
         back_w(last, 0)
         core_send(1)
+        for k in range(2, n):
+            back_w(last, k - 1)
+            core_send(k)
         ones = jnp.ones((8, 128), f32)
         gs[104:112, :] = lax.dot_general(ones, bacc[...], NT, precision=lax.Precision.HIGHEST, preferred_element_type=f32)
         core_send(0)
-        for k in range(2, n):
-            back_w(last, k - 1)
-            core_send(k)
         def st_out(k):
             pend["ac", k].wait_recv()
-        steps = {0: st_core, 1: st_1, 2: st_2, 3: st_z, 4: st_ag2, 5: st_ag1, 6: st_agc, 7: st_out}
+        big = (st_core, st_1, st_2, st_z, st_ag2, st_ag1, st_agc, st_out)
+        small = (small_0, small_1, small_2, small_3, small_4, small_5, lambda: st_out(0))
         for stage, k in ORDER:
             if stage == 9:
                 late(k)
             else:
-                steps[stage](k)
+                if k == 0:
+                    small[stage]()
+                else:
+                    big[stage](k)
         for cp in sends:
             cp.wait_send()
         def finish(q, _):
@@ -332,11 +345,11 @@
                V((NQ, 104, W2), f32), V((NQ, 104, W2), f32), V((NQ, 104, W2), f32), V((NQ, 104, W2), f32),
                V((NQ, 128, W2), bf16), V((1024, 128), f32), V((1024, 1024), f32), V((128, 1024), f32)]
     scratch += [V((NC, half, 1024), f32), V((128, 512), f32), V((128, 512), f32),
-               V((NC, 2, 3, 4 * pr, 512), f32), V((2, 3, 32, 256), f32), V((NC, 2, 4 * pr, 512), f32), V((2, 32, 256), f32),
-               V((NC, 2, 3, pr, 512), f32), V((2, 3, 8, 256), f32), V((NC, pr, 1024), f32), V((8, 512), f32),
-               V((NC, 7, pr, 128), f32), V((7, 8, 512), f32)]
+                V((NC, 2, 3, 4 * pr, 512), f32), V((NC, 2, 4 * pr, 512), f32), V((NC, 2, 3, pr, 512), f32),
+                V((NC, pr, 1024), f32), V((NC, 7, pr, 128), f32),
+                V((7, 16, 512), f32), V((16, 512), f32), V((3, 16, 128), f32), V((4, 16, 128), f32)]
     scratch += [D((NQ, 2)), D((6,))] + [D((NQ,))] * 6
-    for shp in ((n,), (n, 2, 3), (n, 2, 3), (n, 7), (n, 7), (n, 2, 3), (n, 2, 3), (n,)):
+    for shp in ((n,), (n, 2, 3), (n, 2, 3), (n, 7), (n, 7), (n, 2, 3), (n, 2, 3), (n,), (7,), (3,), (3,), (3,), (7,)):
         scratch += [D(shp), D(shp)]
     vm = pl.BlockSpec(memory_space=pltpu.VMEM)
     hbm = pl.BlockSpec(memory_space=pl.ANY)

time: 91.1 us -> 88.3 us (0.969)
  Pallas kernels: 90.4 us -> 87.6 us
    pallas_call x1, Pallas kernels: 86.2 us -> 83.4 us  [per_device(): ghs, ow, os = make_kernel(members, pair_coef, scale)(*args)]
where the time goes in v5:
time: 88.3 us; the launch traced here: 88.2 us
  Pallas kernels  87.6 us (99%)
    pallas_call x1, Pallas kernels, per_device(): ghs, ow, os = make_kernel(members, pair_coef, scale)(*args)  83.4 us
    pallas_call x1, Pallas kernels, place(): pl.pallas_call(kern, out_shape=(jax.ShapeDtypeStruct((2, 1024, 1024), bf1...  4.14 us

profile of v5, /device:TPU:1, one launch (start us, length us, event | category | flops | bytes accessed | tf_op | source)
XLA Modules:
  0.0 88.2 jit_solution(3611876494827295180)
XLA Ops:
  0.6 83.4 %fused.1 = (bf16[2,1024,1024]{2,1,0:T(8,128)(2,1)S(1)}, f32[1024,1024]{1,0:T(8,128)S(1)}, f32[128,1024]{1,0:T(8,128)S(1)}) custom-call(bf16[2,1024,1024]{2,1,0:T(8,128)(2,1)} %hid_hbm.1, bf16[1024,1024]{1,0:T(8,128)(2,1)} %w_hbm.1, f32[1,1024]{1,0:T(1,128)} %bitcast.4, bf16[100,1024]{1,0:T(8,128)(2,1)} %wo_hbm.1, f32[100,1024]{1,0:T(8,128)} %tgt_hbm.1, ...), custom_call_target="tpu_custom_call" | custom-call | tf_op jit(solution)/shard_map/fused/pallas_call | solution.py:387
  84.1 4.1 %place.1 = (bf16[2,1024,1024]{2,1,0:T(8,128)(2,1)}, f32[1024,1024]{1,0:T(8,128)}, f32[100,1024]{1,0:T(8,128)}, f32[1,1024]{1,0:T(1,128)}) custom-call(bf16[2,1024,1024]{2,1,0:T(8,128)(2,1)S(1)} %get-tuple-element.11.ghs, f32[1024,1024]{1,0:T(8,128)S(1)} %get-tuple-element.12.ow, f32[128,1024]{1,0:T(8,128)S(1)} %get-tuple-element.13.os), custom_call_target="tpu_custom_call" | custom-call | tf_op jit(solution)/shard_map/place/pallas_call | solution.py:374

commit v6 on v5

--- a/solution.py
+++ b/solution.py
@@ -44,7 +44,7 @@
     n = NC + 1
 
     def kern(hid_hbm, w_hbm, b_hbm, wo_hbm, tgt_hbm, area_hbm, vw_hbm, ghs, ow, os,
-             w, brow, wo_in, tgt_in, area, vwrow, hid, wo, wot, bcol, vw, tgt, act, slope, pred, pc, px, py, gp, bacc, gw, gs,
+             w, brow, wo_in, tgt_in, area, vwrow, glast, hid, wo, wot, bcol, vw, tgt, act, slope, pred, pc, px, py, gp, bacc, gw, gs,
              rcw, rcs, as_, r1w, b1w, r2w, zw, rzw, rzs, zs, rxs, rys,
              q_h, q_in, s_x, q_x, s_p, q_p, s_f, q_f,
              s_c, q_c, s_1, q_1, s_2, q_2, s_z, q_z, s_az, q_az, s_a2, q_a2, s_a1, q_a1, s_ac, q_ac,
@@ -237,14 +237,17 @@
             g = wts * (smooth_sign(d) * (1.0 / members) - pair_coef * pairs)
             gp[q] = jnp.concatenate([g, jnp.zeros((24, 2 * CQ), f32)], axis=0).astype(bf16)
 
+        def pre_rows(q, rows):
+            g = (dot(wot[rows, :], gp[q]) * slope[q, rows, :]).astype(bf16)
+            gf = g.astype(f32)
+            bacc[rows, :] += gf[:, :128] + gf[:, 128:]
+            return g
+
         def back_pre(q):
             gs[:104, :] += dot_nt(gp[q], act[q])[:104]
             for o in range(4):
                 rows = pl.ds(o * 256, 256)
-                g = (dot(wot[rows, :], gp[q]) * slope[q, rows, :]).astype(bf16)
-                act[q, rows, :] = g
-                gf = g.astype(f32)
-                bacc[rows, :] += gf[:, :128] + gf[:, 128:]
+                act[q, rows, :] = pre_rows(q, rows)
 
         def back_w(q, o):
             rows = pl.ds(o * 256, 256)
@@ -261,21 +264,12 @@
                 for i in range(2):
                     ghs[i, rows, pl.ds(q * CQ, CQ)] = g[:, i * CQ:(i + 1) * CQ]
 
-        gw[...] = jnp.zeros((1024, 1024), f32)
-        bacc[...] = jnp.zeros((1024, 128), f32)
-        for cp in small_in[:5]:
-            cp.wait()
+        small_in[0].wait()
         bcol[...] = jnp.broadcast_to(brow[...], (128, 1024)).T
-        vw[...] = jnp.zeros((128, 128), f32)
-        vw[:, :100] = jnp.broadcast_to(vwrow[...], (128, 100))
-        vw[...] = vw[...].T
-        tgt[96:104, :] = jnp.zeros((8, 1024), f32)
-        tgt[:100, :] = tgt_in[...]
+        small_in[2].wait()
         gs[...] = jnp.zeros((128, 1024), f32)
         gs[:100, :] = wo_in[...].astype(f32)
         wo[...] = gs[...].astype(bf16)
-        wot[...] = gs[...].T.astype(bf16)
-        gs[...] = jnp.zeros((128, 1024), f32)
         small_in[5].wait()
 
         def fwd_step(q, _):
@@ -291,26 +285,40 @@
         def hand_on(q):
             cp_x(q).wait_recv()
             cp_f(q).start()
+        hand_on(0)
+        wot[...] = gs[...].T.astype(bf16)
+        gs[...] = jnp.zeros((128, 1024), f32)
+        gw[...] = jnp.zeros((1024, 1024), f32)
+        bacc[...] = jnp.zeros((1024, 128), f32)
+        for i in (1, 3, 4):
+            small_in[i].wait()
+        vw[...] = jnp.zeros((128, 128), f32)
+        vw[:, :100] = jnp.broadcast_to(vwrow[...], (128, 100))
+        vw[...] = vw[...].T
+        tgt[96:104, :] = jnp.zeros((8, 1024), f32)
+        tgt[:100, :] = tgt_in[...]
+
         def arrive(q):
             cp_p(q).wait_recv()
             cp_f(q).wait_recv()
             grad_pred(q)
-            back_pre(q)
         def bwd_step(q, _):
             arrive(q)
+            back_pre(q)
             hand_on(q + 1)
             for o in range(4):
                 back_w(q, o)
             return 0
-        hand_on(0)
         lax.fori_loop(0, NQ - 1, bwd_step, 0)
         last = NQ - 1
         arrive(last)
-        back_w(last, 0)
-        core_send(1)
-        for k in range(2, n):
-            back_w(last, k - 1)
-            core_send(k)
+        for o in range(4):
+            rows = pl.ds(o * 256, 256)
+            glast[rows, :] = pre_rows(last, rows)
+            gw[rows, :] += dot_nt(glast[rows, :], hid[last])
+            core_send(o + 1)
+        gs[:104, :] += dot_nt(gp[last], act[last])[:104]
+        act[last] = glast[...]
         ones = jnp.ones((8, 128), f32)
         gs[104:112, :] = lax.dot_general(ones, bacc[...], NT, precision=lax.Precision.HIGHEST, preferred_element_type=f32)
         core_send(0)
@@ -338,7 +346,7 @@
     V = pltpu.VMEM
     D = pltpu.SemaphoreType.DMA
     W2 = 2 * CQ
-    scratch = [V((1024, 1024), bf16), V((1, 1024), f32), V((100, 1024), bf16), V((100, 1024), f32), V((1, 1024), f32), V((1, 100), f32),
+    scratch = [V((1024, 1024), bf16), V((1, 1024), f32), V((100, 1024), bf16), V((100, 1024), f32), V((1, 1024), f32), V((1, 100), f32), V((1024, W2), bf16),
                V((NQ, 1024, W2), bf16), V((128, 1024), bf16), V((1024, 128), bf16),
                V((1024, 128), f32), V((128, 128), f32), V((104, 1024), f32),
                V((NQ, 1024, W2), bf16), V((NQ, 1024, W2), f32),

time: 88.3 us -> 89 us (level)
  no operation moved by 1% of the time
where the time goes in v6:
time: 89 us; the launch traced here: 88.9 us
  Pallas kernels  88.3 us (99%)
    pallas_call x1, Pallas kernels, per_device(): ghs, ow, os = make_kernel(members, pair_coef, scale)(*args)  84.1 us
    pallas_call x1, Pallas kernels, place(): pl.pallas_call(kern, out_shape=(jax.ShapeDtypeStruct((2, 1024, 1024), bf1...  4.14 us

profile of v6, /device:TPU:1, one launch (start us, length us, event | category | flops | bytes accessed | tf_op | source)
XLA Modules:
  0.0 88.9 jit_solution(1781209867869608132)
XLA Ops:
  0.6 84.1 %fused.1 = (bf16[2,1024,1024]{2,1,0:T(8,128)(2,1)S(1)}, f32[1024,1024]{1,0:T(8,128)S(1)}, f32[128,1024]{1,0:T(8,128)S(1)}) custom-call(bf16[2,1024,1024]{2,1,0:T(8,128)(2,1)} %hid_hbm.1, bf16[1024,1024]{1,0:T(8,128)(2,1)} %w_hbm.1, f32[1,1024]{1,0:T(1,128)} %bitcast.4, bf16[100,1024]{1,0:T(8,128)(2,1)} %wo_hbm.1, f32[100,1024]{1,0:T(8,128)} %tgt_hbm.1, ...), custom_call_target="tpu_custom_call" | custom-call | tf_op jit(solution)/shard_map/fused/pallas_call | solution.py:395
  84.8 4.1 %place.1 = (bf16[2,1024,1024]{2,1,0:T(8,128)(2,1)}, f32[1024,1024]{1,0:T(8,128)}, f32[100,1024]{1,0:T(8,128)}, f32[1,1024]{1,0:T(1,128)}) custom-call(bf16[2,1024,1024]{2,1,0:T(8,128)(2,1)S(1)} %get-tuple-element.11.ghs, f32[1024,1024]{1,0:T(8,128)S(1)} %get-tuple-element.12.ow, f32[128,1024]{1,0:T(8,128)S(1)} %get-tuple-element.13.os), custom_call_target="tpu_custom_call" | custom-call | tf_op jit(solution)/shard_map/place/pallas_call | solution.py:382
